TPU v7x, 32 devices: a whole 2x2x4 slice. The times are simulated.
32 devices in a mesh: member: 2 (over x), horiz: 16 (over z, y, core).
Axes of the slice: x: 2, y: 2, z: 4, core: 2. Of those that a mesh axis runs over, the one named last changes fastest.
Arguments:
- perturbation: float32 [16, 80, 4, 1920], P('member', 'horiz'), parts along dimension 0, may hold values from -36 to 36
- base_state: float32 [8, 80, 4, 1920], P(None, 'horiz'), may hold values from -6 to 6
- target_state: float32 [8, 80, 4, 1920], P(None, 'horiz'), may hold values from -6 to 6
- cost_weight: float32 [80, 1920], P('horiz'), may hold values from 0.5 to 6
- diffusivity: float32 [80, 1920], P('horiz'), may hold values from 0.04 to 0.2
- chan_mix: float32 [8, 4, 4], replicated, may hold values from -3 to 3
- coupler_mix: float32 [4, 4], replicated, may hold values from -3 to 3
- owner_mix: float32 [16, 80, 80], P('horiz'), may hold values from -0.625 to 0.625
- air_temp: float32 [2, 16, 80, 128], P(None, 'horiz'), may hold values from -6 to 6
- wind_speed: float32 [2, 16, 80, 128], P(None, 'horiz'), may hold values from 2 to 12
- wet_list: int32 [16, 75], P('horiz'), may hold values from -1 to 74, as said below
- wet_owner: int32 [16, 75], P('horiz'), may hold values from -1 to 15, as said below
- remap_src: int32 [240], P('horiz'), may hold values from 0 to 79, as said below
- remap_tgt: int32 [240], P('horiz'), may hold values from 0 to 31, as said below
- remap_weight: float32 [240], P('horiz'), may hold values from 0.2 to 0.8
Outputs:
- new_perturbation: float32 [16, 80, 4, 1920], P('member', 'horiz'), parts along dimension 0
There are 2 independent parts, one for each index of `member`. A program takes and returns all parts, laid end to end along the dimension named above; an argument that names none is the same for every part. Nothing has to cross between parts.
Inputs may be any that keep to these rules, and one draw needn't show every extreme that they name: Each row of wet_list names distinct tiles, valid entries first and -1 after them; wet_owner is -1 exactly where wet_list is. Every device lists at least 37 wet tiles and some device lists all 75. Within one device's list no owner appears more than 5 times, and some owner appears exactly 5 times in every device's list. `wet_owner`: see wet_list. `remap_src`: the source row of each entry is one of the rows of the device that holds the entry. `remap_tgt`: each entry's latitude row differs from (2 times its source row) // 5 by at most 1.
All inputs are finite; a program needn't handle non-finite values.
Results may differ from a plain program's by a relative error of at most 0.0001.
Values sent between devices are 32-bit elements; how exact they have to be, the bound alone decides.
A program may use at most 64 MiB of HBM per device.

v0:
```python
import jax
import jax.numpy as jnp
from jax import lax
from jax.sharding import PartitionSpec as P

LAT_DEV = 2


KAPPA_V = 0.1
TIME_STEP = 0.3
FLUX_RATE = 0.05
FEEDBACK = 0.5
ASCENT = 0.5
EPSILON = 1e-06
HIGHEST = lax.Precision.HIGHEST


def with_halo(block, sides, width):
    for axis, dim in sides:
        count = lax.axis_size(axis)
        forward = [(i, i + 1) for i in range(count - 1)]
        backward = [(target, source) for source, target in forward]
        low = lax.ppermute(
            lax.slice_in_dim(block, block.shape[dim] - width, None, axis=dim), axis, forward
        )
        high = lax.ppermute(lax.slice_in_dim(block, 0, width, axis=dim), axis, backward)
        block = jnp.concatenate([low, block, high], axis=dim)
    return block


def channel_drive(ocean_field, chan_mix):
    return jnp.tanh(jnp.einsum("lck,ljkx->ljcx", chan_mix, ocean_field, precision=HIGHEST))


def level_diff(ocean_field):
    padded = jnp.pad(ocean_field, ((1, 1), (0, 0), (0, 0), (0, 0)))
    return padded[2:] + padded[:-2] - 2.0 * ocean_field


def horiz_lap(ocean_field):
    padded = with_halo(ocean_field, (("horiz", 1),), 1)
    return (
        padded[:, 2:]
        + padded[:, :-2]
        + jnp.roll(ocean_field, -1, axis=3)
        + jnp.roll(ocean_field, 1, axis=3)
        - 4.0 * ocean_field
    )


def owner_flux(arrived, air_field, wind_field, mixing, coupler_mix):
    cell_shape = arrived.shape
    flat = arrived.reshape((cell_shape[0] * cell_shape[1],) + cell_shape[2:])
    mixed = jnp.tanh(jnp.einsum("pq,qcx->pcx", mixing, flat, precision=HIGHEST))
    air_flat = air_field.reshape(flat.shape[0], flat.shape[2])
    wind_flat = wind_field.reshape(flat.shape[0], flat.shape[2])
    contrast = (
        jnp.concatenate([(air_flat - flat[:, 0, :])[:, None, :], flat[:, 1:, :]], axis=1) + mixed
    )
    forcing = jnp.einsum("ck,pkx->pcx", coupler_mix, contrast, precision=HIGHEST)
    return (FLUX_RATE * wind_flat[:, None, :] * jnp.tanh(forcing)).reshape(cell_shape)


def flux_cotangent(arrived, cotangent, air_field, wind_field, mixing, coupler_mix):

    def forward_flux(values):
        return owner_flux(values, air_field, wind_field, mixing, coupler_mix)

    _, pullback = jax.vjp(forward_flux, arrived)
    return pullback(cotangent)[0]


def to_tiles(surface, tile_width):
    row_count, channels, cells = surface.shape
    pieces = surface.reshape(row_count, channels, cells // tile_width, tile_width).transpose(
        0, 2, 1, 3
    )
    return pieces.reshape(row_count * (cells // tile_width), channels, tile_width)


def from_tiles(tile_view, row_count):
    tile_total, channels, tile_width = tile_view.shape
    per_row = tile_total // row_count
    pieces = tile_view.reshape(row_count, per_row, channels, tile_width).transpose(0, 2, 1, 3)
    return pieces.reshape(row_count, channels, per_row * tile_width)


def route_tables(wet_row, owner_row, device_count, capacity):
    live_mask = owner_row >= 0
    onehot = (owner_row[:, None] == jnp.arange(device_count, dtype=jnp.int32)[None, :]).astype(
        jnp.int32
    )
    earlier = jnp.cumsum(onehot, axis=0) - onehot
    slot_rank = jnp.sum(earlier * onehot, axis=1)
    slot_index = jnp.where(live_mask, owner_row * capacity + slot_rank, -1)
    tile_safe = jnp.where(live_mask, wet_row, 0)
    return (live_mask, slot_index, tile_safe)


def owner_round(picked, slot_index, live_mask, device_count, capacity, owner_work):
    entry_count = picked.shape[0]
    slot_total = device_count * capacity
    select = (slot_index[None, :] == jnp.arange(slot_total, dtype=jnp.int32)[:, None]).astype(
        jnp.float32
    )
    packed = jnp.dot(
        select,
        picked.reshape(entry_count, -1),
        precision=HIGHEST,
        preferred_element_type=jnp.float32,
    )
    outgoing = packed.reshape((device_count, capacity) + picked.shape[1:])
    arrived = lax.all_to_all(outgoing, "horiz", split_axis=0, concat_axis=0, tiled=True)
    result = owner_work(arrived)
    returned = lax.all_to_all(result, "horiz", split_axis=0, concat_axis=0, tiled=True)
    flattened = returned.reshape(slot_total, -1)
    taken = flattened[jnp.maximum(slot_index, 0)] * live_mask.astype(jnp.float32)[:, None]
    return (taken.reshape((entry_count,) + result.shape[2:]), arrived)


def unpack_tiles(values, tile_safe, live_mask, tile_total):
    select = (
        (tile_safe[None, :] == jnp.arange(tile_total, dtype=jnp.int32)[:, None])
        & live_mask[None, :]
    ).astype(jnp.float32)
    placed = jnp.dot(
        select,
        values.reshape(values.shape[0], -1),
        precision=HIGHEST,
        preferred_element_type=jnp.float32,
    )
    return placed.reshape((tile_total,) + values.shape[1:])


def remap_cycle(surface, source_local, remap_tgt, remap_weight, lat_rows, middle):
    row_count = surface.shape[0]
    weighted = surface[source_local] * remap_weight[:, None]
    source_select = (
        source_local[None, :] == jnp.arange(row_count, dtype=jnp.int32)[:, None]
    ).astype(jnp.float32)
    first_lat = lax.axis_index("horiz") * lat_rows - 1
    select_rows = (
        remap_tgt[None, :] - first_lat == jnp.arange(lat_rows + 2, dtype=jnp.int32)[:, None]
    ).astype(jnp.float32)
    local_sums = jnp.dot(
        select_rows, weighted, precision=HIGHEST, preferred_element_type=jnp.float32
    )
    edge_rows = jnp.stack([local_sums[0], local_sums[-1]])
    bordered = with_halo(edge_rows, (("horiz", 0),), 1)
    own_rows = local_sums[1:-1]
    own_rows = own_rows.at[0].add(bordered[0]).at[-1].add(bordered[-1])
    processed, stored = middle(own_rows)
    extended = with_halo(processed, (("horiz", 0),), 1)
    at_targets = jnp.dot(
        select_rows.T, extended, precision=HIGHEST, preferred_element_type=jnp.float32
    )
    at_targets = at_targets * remap_weight[:, None]
    returned = jnp.dot(
        source_select, at_targets, precision=HIGHEST, preferred_element_type=jnp.float32
    )
    return (returned, stored)


def forward_middle(summed):
    atmos = jnp.tanh(summed)
    return (atmos, atmos)


def body(
    perturbation,
    base_state,
    target_state,
    cost_weight,
    diffusivity,
    chan_mix,
    coupler_mix,
    owner_mix,
    air_temp,
    wind_speed,
    wet_list,
    wet_owner,
    remap_src,
    remap_tgt,
    remap_weight,
):
    device_count = lax.axis_size("horiz")
    row_count = base_state.shape[1]
    capacity = air_temp.shape[2] // device_count
    tile_total = wet_list.shape[1]
    hour_count = air_temp.shape[0]
    tile_width = air_temp.shape[3]
    mixing = owner_mix[0]
    live_mask, slot_index, tile_safe = route_tables(
        wet_list[0], wet_owner[0], device_count, capacity
    )
    source_local = remap_src - lax.axis_index("horiz") * row_count
    coeff_field = diffusivity[None, :, None, :]
    ocean_field = base_state + perturbation
    saved = []
    for hour_index in range(hour_count):
        start_field = ocean_field
        drive = channel_drive(ocean_field, chan_mix)
        ocean_field = (
            ocean_field
            + coeff_field * horiz_lap(ocean_field)
            + KAPPA_V * level_diff(ocean_field)
            + TIME_STEP * drive
        )
        picked = (
            to_tiles(ocean_field[0], tile_width)[tile_safe]
            * live_mask.astype(jnp.float32)[:, None, None]
        )
        air_now = air_temp[hour_index, 0].reshape(device_count, capacity, tile_width)
        wind_now = wind_speed[hour_index, 0].reshape(device_count, capacity, tile_width)

        def flux_work(arrived, air_now=air_now, wind_now=wind_now):
            return owner_flux(arrived, air_now, wind_now, mixing, coupler_mix)

        flux_entries, arrived = owner_round(
            picked, slot_index, live_mask, device_count, capacity, flux_work
        )
        flux_tiles = unpack_tiles(flux_entries, tile_safe, live_mask, tile_total)
        ocean_field = ocean_field.at[0].add(from_tiles(flux_tiles, row_count))
        returned, atmos = remap_cycle(
            ocean_field[0, :, 0, :], source_local, remap_tgt, remap_weight, LAT_DEV, forward_middle
        )
        ocean_field = ocean_field.at[0, :, 0, :].add(FEEDBACK * returned)
        saved.append((start_field, drive, picked, arrived, atmos, air_now, wind_now))
    adjoint = (cost_weight * cost_weight)[None, :, None, :] * (ocean_field - target_state)
    for hour_index in reversed(range(hour_count)):
        start_field, drive, picked, arrived, atmos, air_now, wind_now = saved[hour_index]

        def adjoint_middle(summed, atmos=atmos):
            return (summed * (1.0 - atmos * atmos), atmos)

        surface_cot, _ = remap_cycle(
            FEEDBACK * adjoint[0, :, 0, :],
            source_local,
            remap_tgt,
            remap_weight,
            LAT_DEV,
            adjoint_middle,
        )
        adjoint = adjoint.at[0, :, 0, :].add(surface_cot)
        cot_entries = to_tiles(adjoint[0], tile_width)[tile_safe]

        def cot_work(got, arrived=arrived, air_now=air_now, wind_now=wind_now):
            return flux_cotangent(arrived, got, air_now, wind_now, mixing, coupler_mix)

        back_entries, _ = owner_round(
            cot_entries, slot_index, live_mask, device_count, capacity, cot_work
        )
        back_tiles = unpack_tiles(back_entries, tile_safe, live_mask, tile_total)
        adjoint = adjoint.at[0].add(from_tiles(back_tiles, row_count))
        adjoint = (
            adjoint
            + horiz_lap(coeff_field * adjoint)
            + KAPPA_V * level_diff(adjoint)
            + TIME_STEP
            * jnp.einsum(
                "lck,ljcx->ljkx", chan_mix, (1.0 - drive * drive) * adjoint, precision=HIGHEST
            )
        )
    cell_total = adjoint.size * device_count
    statistics = lax.psum(
        (
            jnp.sum(perturbation * perturbation),
            jnp.sum(perturbation * adjoint),
            jnp.sum(adjoint * adjoint),
        ),
        "horiz",
    )
    mean_pp = statistics[0] / cell_total
    mean_pg = statistics[1] / cell_total
    mean_gg = statistics[2] / cell_total
    grad_scale = lax.rsqrt(mean_gg + EPSILON)
    mean_sq = (
        mean_pp
        + 2.0 * ASCENT * grad_scale * mean_pg
        + ASCENT * ASCENT * grad_scale * grad_scale * mean_gg
    )
    stepped = perturbation + ASCENT * grad_scale * adjoint
    return stepped * lax.rsqrt(mean_sq + EPSILON)


def solution(mesh):
    placed = (
        P("member", "horiz", None, None),
        P(None, "horiz", None, None),
        P(None, "horiz", None, None),
        P("horiz", None),
        P("horiz", None),
        P(),
        P(),
        P("horiz", None, None),
        P(None, "horiz", None, None),
        P(None, "horiz", None, None),
        P("horiz", None),
        P("horiz", None),
        P("horiz"),
        P("horiz"),
        P("horiz"),
    )
    return jax.shard_map(
        body,
        mesh=mesh,
        in_specs=placed,
        out_specs=P("member", "horiz", None, None),
        check_vma=False,
    )
```

profile of v0, /device:TPU:0, one launch (start us, length us, event | category | flops | bytes accessed | tf_op | source)
XLA Modules:
  0.0 295.6 jit_solution(9869927661100436124)
XLA Ops:
  0.0 1.8 copy_add_fusion
  3.2 3.2 %collective-permute-start.1 = (f32[8,1,4,1920]{3,0,2,1:T(8,128)S(1)}, f32[8,1,4,1920]{3,0,2,1:T(8,128)S(1)}, u32[]{:S(2)}, u32[]{:S(2)}) collective-permute-start(f32[8,1,4,1920]{3,0,2,1:T(8,128)S(1)} %get-tuple-element.234), channel_id=1, source_target_pairs={{0,1},{1,2},{2,3},{3,4},{4,5},{5,6},{6,7},{7,8},{8,9},{9,10},{10,1... | collective-permute-start | bytes 737288 | tf_op jit(solution)/shard_map/ppermute | solution.py:23
  6.4 1.9 fusion.217
  8.8 3.3 %fusion.51 = f32[8,5,1920,4]{2,3,1,0:T(4,128)} fusion(f32[8,4,4,1]{1,2,3,0:T(4,128)S(1)} %copy.229, f32[8,5,4,1920]{3,0,2,1:T(8,128)S(1)} %copy_add_fusion), kind=kOutput, calls=%fused_computation.92 | convolution fusion | flops 14745600 | bytes 2458112 | tf_op jit(solution)/shard_map/lck,ljkx->ljcx/dot_general | solution.py:32
  12.3 2.9 fusion.6
  19.0 7.9 %all-to-all-start = ((f32[16,5,4,128]{3,2,1,0:T(4,128)}), f32[16,5,4,128]{3,2,1,0:T(4,128)S(1)}, u32[]{:S(2)}, u32[]{:S(2)}) async-start(f32[16,5,4,128]{3,2,1,0:T(4,128)} %copy.175), calls=%async_computation | async-start | bytes 327680 | tf_op jit(solution)/shard_map/all_to_all | solution.py:113
  27.6 7.8 %all-to-all-done = f32[16,5,4,128]{3,2,1,0:T(4,128)S(1)} async-done(((f32[16,5,4,128]{3,2,1,0:T(4,128)}), f32[16,5,4,128]{3,2,1,0:T(4,128)S(1)}, u32[]{:S(2)}, u32[]{:S(2)}) %all-to-all-start) | async-done | bytes 163872 | tf_op jit(solution)/shard_map/all_to_all | solution.py:113
  36.9 3.5 %all-to-all-start.1 = ((f32[16,5,4,128]{3,2,1,0:T(4,128)}), f32[16,5,4,128]{3,2,1,0:T(4,128)S(1)}, u32[]{:S(2)}, u32[]{:S(2)}) async-start(f32[16,5,4,128]{3,2,1,0:T(4,128)} %bitcast.25), calls=%async_computation.1 | async-start | bytes 327680 | tf_op jit(solution)/shard_map/all_to_all | solution.py:115
  40.5 8.4 %all-to-all-done.1 = f32[16,5,4,128]{3,2,1,0:T(4,128)S(1)} async-done(((f32[16,5,4,128]{3,2,1,0:T(4,128)}), f32[16,5,4,128]{3,2,1,0:T(4,128)S(1)}, u32[]{:S(2)}, u32[]{:S(2)}) %all-to-all-start.1) | async-done | bytes 163872 | tf_op jit(solution)/shard_map/all_to_all | solution.py:115
  53.7 1.6 collective-permute-done.3
  55.5 3.8 %collective-permute-start.4 = (f32[1,1920]{1,0:T(1,128)S(1)}, f32[1,1920]{1,0:T(1,128)S(1)}, u32[]{:S(2)}, u32[]{:S(2)}) collective-permute-start(f32[1,1920]{1,0:T(1,128)S(1)} %get-tuple-element.251), channel_id=1, source_target_pairs={{0,1},{1,2},{2,3},{3,4},{4,5},{5,6},{6,7},{7,8},{8,9},{9,10},{10,1... | collective-permute-start | bytes 23048 | tf_op jit(solution)/shard_map/ppermute | solution.py:23
  60.8 2.8 scatter-add.54
  66.2 4.1 %collective-permute-start.7 = (f32[8,1,4,1920]{3,0,2,1:T(8,128)S(1)}, f32[8,1,4,1920]{3,0,2,1:T(8,128)S(1)}, u32[]{:S(2)}, u32[]{:S(2)}) collective-permute-start(f32[8,1,4,1920]{3,0,2,1:T(8,128)S(1)} %get-tuple-element.228), channel_id=1, source_target_pairs={{0,1},{1,2},{2,3},{3,4},{4,5},{5,6},{6,7},{7,8},{8,9},{9,10},{10,1... | collective-permute-start | bytes 737288 | tf_op jit(solution)/shard_map/ppermute | solution.py:23
  70.3 2.3 fusion.49
  72.7 1.9 fusion.11
  74.6 1.7 slice_reduce_fusion.2
  77.8 18.7 %all_to_all.40 = f32[16,5,4,128]{3,2,1,0:T(4,128)S(1)} all-to-all(f32[16,5,4,128]{3,2,1,0:T(4,128)S(1)} %copy.189), channel_id=1, replica_groups=mesh['member'=2,'horiz'=16] {'horiz'}, dimensions={0} | all-to-all | bytes 327680 | tf_op jit(solution)/shard_map/all_to_all | solution.py:113
  97.3 11.1 %all_to_all.41 = f32[16,5,4,128]{3,2,1,0:T(4,128)S(1)} all-to-all(f32[16,5,4,128]{3,2,1,0:T(4,128)S(1)} %bitcast.281), channel_id=1, replica_groups=mesh['member'=2,'horiz'=16] {'horiz'}, dimensions={0} | all-to-all | bytes 327680 | tf_op jit(solution)/shard_map/all_to_all | solution.py:115
  109.8 1.5 slice_add_fusion.2
  115.0 1.6 collective-permute-done.9
  116.8 3.8 %collective-permute-start.10 = (f32[1,1920]{1,0:T(1,128)S(1)}, f32[1,1920]{1,0:T(1,128)S(1)}, u32[]{:S(2)}, u32[]{:S(2)}) collective-permute-start(f32[1,1920]{1,0:T(1,128)S(1)} %get-tuple-element.249), channel_id=1, source_target_pairs={{0,1},{1,2},{2,3},{3,4},{4,5},{5,6},{6,7},{7,8},{8,9},{9,10},{10,1... | collective-permute-start | bytes 23048 | tf_op jit(solution)/shard_map/ppermute | solution.py:23
  122.0 3.3 %scatter-add.60 = f32[8,5,4,1920]{3,0,2,1:T(8,128)} dynamic-update-slice(f32[8,5,4,1920]{3,0,2,1:T(8,128)} %fusion.11, f32[1,5,4,1920]{3,0,2,1:T(1,128)S(1)} %slice_add_fusion.2, s32[]{:T(128)} %constant.398.clone.1, s32[]{:T(128)} %constant.398.clone.1, s32[]{:T(128)} %constant.398.clone.1, s32[]{:T(128)} %constant.398.clone.1) | dynamic-update-slice | bytes 307204 | tf_op jit(solution)/shard_map/scatter-add | solution.py:223
  125.7 1.8 scatter-add.65
  127.5 1.8 fusion.48
  130.4 3.0 %collective-permute-start.12 = (f32[1,1920]{1,0:T(1,128)S(1)}, f32[1,1920]{1,0:T(1,128)S(1)}, u32[]{:S(2)}, u32[]{:S(2)}) collective-permute-start(f32[1,1920]{1,0:T(1,128)S(1)} %get-tuple-element.240), channel_id=1, source_target_pairs={{0,1},{1,2},{2,3},{3,4},{4,5},{5,6},{6,7},{7,8},{8,9},{9,10},{10,1... | collective-permute-start | bytes 23048 | tf_op jit(solution)/shard_map/ppermute | solution.py:23
  134.9 3.1 %collective-permute-done.13 = f32[1,1920]{1,0:T(1,128)S(1)} collective-permute-done((f32[1,1920]{1,0:T(1,128)S(1)}, f32[1,1920]{1,0:T(1,128)S(1)}, u32[]{:S(2)}, u32[]{:S(2)}) %collective-permute-start.13) | collective-permute-done | bytes 7712 | tf_op jit(solution)/shard_map/ppermute | solution.py:26
  138.1 4.3 %collective-permute-start.14 = (f32[1,1920]{1,0:T(1,128)S(1)}, f32[1,1920]{1,0:T(1,128)S(1)}, u32[]{:S(2)}, u32[]{:S(2)}) collective-permute-start(f32[1,1920]{1,0:T(1,128)S(1)} %get-tuple-element.247), channel_id=1, source_target_pairs={{0,1},{1,2},{2,3},{3,4},{4,5},{5,6},{6,7},{7,8},{8,9},{9,10},{10,1... | collective-permute-start | bytes 23048 | tf_op jit(solution)/shard_map/ppermute | solution.py:23
  143.8 1.8 collective-permute-done.15
  146.8 1.5 gather_fusion.7
  150.4 17.1 %all_to_all.42 = f32[16,5,4,128]{3,2,1,0:T(4,128)S(1)} all-to-all(f32[16,5,4,128]{3,2,1,0:T(4,128)S(1)} %copy.199), channel_id=1, replica_groups=mesh['member'=2,'horiz'=16] {'horiz'}, dimensions={0} | all-to-all | bytes 327680 | tf_op jit(solution)/shard_map/all_to_all | solution.py:113
  169.2 11.1 %all_to_all.43 = f32[16,5,4,128]{3,2,1,0:T(4,128)S(1)} all-to-all(f32[16,5,4,128]{3,2,1,0:T(4,128)S(1)} %bitcast.297), channel_id=1, replica_groups=mesh['member'=2,'horiz'=16] {'horiz'}, dimensions={0} | all-to-all | bytes 327680 | tf_op jit(solution)/shard_map/all_to_all | solution.py:115
  181.9 2.8 scatter-add.71
  187.5 3.0 %collective-permute-start.17 = (f32[8,1,4,1920]{3,0,2,1:T(8,128)S(1)}, f32[8,1,4,1920]{3,0,2,1:T(8,128)S(1)}, u32[]{:S(2)}, u32[]{:S(2)}) collective-permute-start(f32[8,1,4,1920]{3,0,2,1:T(8,128)S(1)} %get-tuple-element.222), channel_id=1, source_target_pairs={{0,1},{1,2},{2,3},{3,4},{4,5},{5,6},{6,7},{7,8},{8,9},{9,10},{10,1... | collective-permute-start | bytes 737288 | tf_op jit(solution)/shard_map/ppermute | solution.py:23
  190.5 2.3 fusion.46
  194.9 3.9 %collective-permute-start.18 = (f32[1,1920]{1,0:T(1,128)S(1)}, f32[1,1920]{1,0:T(1,128)S(1)}, u32[]{:S(2)}, u32[]{:S(2)}) collective-permute-start(f32[1,1920]{1,0:T(1,128)S(1)} %get-tuple-element.238), channel_id=1, source_target_pairs={{0,1},{1,2},{2,3},{3,4},{4,5},{5,6},{6,7},{7,8},{8,9},{9,10},{10,1... | collective-permute-start | bytes 23048 | tf_op jit(solution)/shard_map/ppermute | solution.py:23
  200.2 3.6 %collective-permute-done.19 = f32[1,1920]{1,0:T(1,128)S(1)} collective-permute-done((f32[1,1920]{1,0:T(1,128)S(1)}, f32[1,1920]{1,0:T(1,128)S(1)}, u32[]{:S(2)}, u32[]{:S(2)}) %collective-permute-start.19) | collective-permute-done | bytes 7712 | tf_op jit(solution)/shard_map/ppermute | solution.py:26
  204.0 4.3 %collective-permute-start.20 = (f32[1,1920]{1,0:T(1,128)S(1)}, f32[1,1920]{1,0:T(1,128)S(1)}, u32[]{:S(2)}, u32[]{:S(2)}) collective-permute-start(f32[1,1920]{1,0:T(1,128)S(1)} %get-tuple-element.245), channel_id=1, source_target_pairs={{0,1},{1,2},{2,3},{3,4},{4,5},{5,6},{6,7},{7,8},{8,9},{9,10},{10,1... | collective-permute-start | bytes 23048 | tf_op jit(solution)/shard_map/ppermute | solution.py:23
  209.6 1.8 collective-permute-done.21
  214.0 15.1 %all_to_all.44 = f32[16,5,4,128]{3,2,1,0:T(4,128)S(1)} all-to-all(f32[16,5,4,128]{3,2,1,0:T(4,128)S(1)} %copy.211), channel_id=1, replica_groups=mesh['member'=2,'horiz'=16] {'horiz'}, dimensions={0} | all-to-all | bytes 327680 | tf_op jit(solution)/shard_map/all_to_all | solution.py:113
  230.7 3.5 %all-to-all-start.7 = ((f32[16,5,4,128]{3,2,1,0:T(4,128)}), f32[16,5,4,128]{3,2,1,0:T(4,128)S(1)}, u32[]{:S(2)}, u32[]{:S(2)}) async-start(f32[16,5,4,128]{3,2,1,0:T(4,128)} %bitcast.73), calls=%async_computation.7 | async-start | bytes 327680 | tf_op jit(solution)/shard_map/all_to_all | solution.py:115
  235.6 7.1 %all-to-all-done.7 = f32[16,5,4,128]{3,2,1,0:T(4,128)S(1)} async-done(((f32[16,5,4,128]{3,2,1,0:T(4,128)}), f32[16,5,4,128]{3,2,1,0:T(4,128)S(1)}, u32[]{:S(2)}, u32[]{:S(2)}) %all-to-all-start.7) | async-done | bytes 163872 | tf_op jit(solution)/shard_map/all_to_all | solution.py:115
  244.2 2.8 scatter-add.79
  247.1 1.5 broadcast_multiply_fusion
  250.3 3.3 %collective-permute-start.23 = (f32[8,1,4,1920]{3,0,2,1:T(8,128)S(1)}, f32[8,1,4,1920]{3,0,2,1:T(8,128)S(1)}, u32[]{:S(2)}, u32[]{:S(2)}) collective-permute-start(f32[8,1,4,1920]{3,0,2,1:T(8,128)S(1)} %get-tuple-element.208), channel_id=1, source_target_pairs={{0,1},{1,2},{2,3},{3,4},{4,5},{5,6},{6,7},{7,8},{8,9},{9,10},{10,1... | collective-permute-start | bytes 737288 | tf_op jit(solution)/shard_map/ppermute | solution.py:23
  253.6 2.3 fusion.44
  256.0 2.8 multiply_reduce_fusion
  258.8 31.9 %all-reduce.8 = (f32[]{:T(128)}, f32[]{:T(128)}, f32[]{:T(128)}) all-reduce(f32[]{:T(128)} %multiply_reduce_fusion.1, f32[]{:T(128)} %get-tuple-element.198, f32[]{:T(128)} %get-tuple-element.197), channel_id=1, replica_groups=mesh['member'=2,'horiz'=16] {'horiz'}, use_global_device_ids=true, to_apply=%region_5.6 | all-reduce | flops 3 | bytes 24 | tf_op jit(solution)/shard_map/psum | solution.py:265
  292.8 1.4 add_multiply_fusion
  (300 shorter events, 53.6 us)
Async XLA Ops:
  0.0 35.4 %copy-start = (f32[1,80,80]{2,1,0:T(8,128)S(1)}, f32[1,80,80]{2,1,0:T(8,128)}, u32[]{:S(2)}) copy-start(f32[1,80,80]{2,1,0:T(8,128)} %param.54) | copy-start | bytes 76804
  1.9 10.4 %collective-permute-start = (f32[8,1,4,1920]{3,0,2,1:T(8,128)S(1)}, f32[8,1,4,1920]{3,0,2,1:T(8,128)S(1)}, u32[]{:S(2)}, u32[]{:S(2)}) collective-permute-start(f32[8,1,4,1920]{3,0,2,1:T(8,128)S(1)} %get-tuple-element.233), channel_id=1, source_target_pairs={{1,0},{2,1},{3,2},{4,3},{5,4},{6,5},{7,6},{8,7},{9,8},{10,9},{11,1... | collective-permute-start | bytes 737288 | tf_op jit(solution)/shard_map/ppermute | solution.py:26
  3.2 9.1 %collective-permute-start.1 = (f32[8,1,4,1920]{3,0,2,1:T(8,128)S(1)}, f32[8,1,4,1920]{3,0,2,1:T(8,128)S(1)}, u32[]{:S(2)}, u32[]{:S(2)}) collective-permute-start(f32[8,1,4,1920]{3,0,2,1:T(8,128)S(1)} %get-tuple-element.234), channel_id=1, source_target_pairs={{0,1},{1,2},{2,3},{3,4},{4,5},{5,6},{6,7},{7,8},{8,9},{9,10},{10,1... | collective-permute-start | bytes 737288 | tf_op jit(solution)/shard_map/ppermute | solution.py:23
  8.2 69.0 %copy-start.21 = (f32[75]{0:T(128)}, f32[75]{0:T(128)S(1)}, u32[]{:S(2)}) copy-start(f32[75]{0:T(128)S(1)} %compare_convert_fusion) | copy-start | bytes 904
  8.7 40.9 %copy-start.24 = (s32[75]{0:T(128)}, s32[75]{0:T(128)S(1)}, u32[]{:S(2)}) copy-start(s32[75]{0:T(128)S(1)} %get-tuple-element.253) | copy-start | bytes 904
  8.7 68.7 %copy-start.27 = (s32[75]{0:T(128)}, s32[75]{0:T(128)S(1)}, u32[]{:S(2)}) copy-start(s32[75]{0:T(128)S(1)} %get-tuple-element.254) | copy-start | bytes 904
  8.7 40.9 %copy-start.35 = (pred[75]{0:T(512)(128)(4,1)}, pred[75]{0:T(512)(128)(4,1)S(1)}, u32[]{:S(2)}) copy-start(pred[75]{0:T(512)(128)(4,1)S(1)} %fusion.194) | copy-start | bytes 229
  8.8 61.5 %copy-start.5 = (f32[8,4,4,1]{1,2,3,0:T(4,128)}, f32[8,4,4,1]{1,2,3,0:T(4,128)S(1)}, u32[]{:S(2)}) copy-start(f32[8,4,4,1]{1,2,3,0:T(4,128)S(1)} %copy.229) | copy-start | bytes 1540
  12.2 51.7 %copy-start.29 = (s32[15]{0:T(128)}, s32[15]{0:T(128)S(1)}, u32[]{:S(2)}) copy-start(s32[15]{0:T(128)S(1)} %get-tuple-element.204) | copy-start | bytes 184
  12.2 64.3 %copy-start.32 = (s32[1024]{0:T(1024)}, s32[1024]{0:T(1024)S(1)}, u32[]{:S(2)}) copy-start(s32[1024]{0:T(1024)S(1)} %pad_clamp_fusion.2) | copy-start | bytes 12292
  17.8 17.6 %copy-start.14 = (f32[2,1,80,128]{3,2,1,0:T(8,128)S(1)}, f32[2,1,80,128]{3,2,1,0:T(8,128)}, u32[]{:S(2)}) copy-start(f32[2,1,80,128]{3,2,1,0:T(8,128)} %param.55) | copy-start | bytes 245764
  18.0 17.8 %copy-start.16 = (f32[4,4]{1,0:T(4,128)S(1)}, f32[4,4]{1,0:T(4,128)}, u32[]{:S(2)}) copy-start(f32[4,4]{1,0:T(4,128)} %param.53) | copy-start | bytes 196
  19.0 16.4 %all-to-all-start = ((f32[16,5,4,128]{3,2,1,0:T(4,128)}), f32[16,5,4,128]{3,2,1,0:T(4,128)S(1)}, u32[]{:S(2)}, u32[]{:S(2)}) async-start(f32[16,5,4,128]{3,2,1,0:T(4,128)} %copy.175), calls=%async_computation | async-start | bytes 327680 | tf_op jit(solution)/shard_map/all_to_all | solution.py:113
  26.9 13.5 %copy-start.42 = (s32[15]{0:T(128)S(1)}, s32[15]{0:T(128)}, u32[]{:S(2)}) copy-start(s32[15]{0:T(128)} %param.60) | copy-start | bytes 184
  26.9 21.9 %copy-start.33 = (s32[1024]{0:T(1024)}, s32[1024]{0:T(1024)S(1)}, u32[]{:S(2)}) copy-start(s32[1024]{0:T(1024)S(1)} %pad_clamp_fusion.1) | copy-start | bytes 12292
  27.6 21.3 %copy-start.7 = (f32[80,128]{1,0:T(8,128)}, f32[80,128]{1,0:T(8,128)S(1)}, u32[]{:S(2)}) copy-start(f32[80,128]{1,0:T(8,128)S(1)} %get-tuple-element.236) | copy-start | bytes 122884
  36.9 12.0 %all-to-all-start.1 = ((f32[16,5,4,128]{3,2,1,0:T(4,128)}), f32[16,5,4,128]{3,2,1,0:T(4,128)S(1)}, u32[]{:S(2)}, u32[]{:S(2)}) async-start(f32[16,5,4,128]{3,2,1,0:T(4,128)} %bitcast.25), calls=%async_computation.1 | async-start | bytes 327680 | tf_op jit(solution)/shard_map/all_to_all | solution.py:115
  40.5 23.2 %copy-start.18 = (s32[15]{0:T(128)}, s32[15]{0:T(128)S(1)}, u32[]{:S(2)}) copy-start(s32[15]{0:T(128)S(1)} %broadcast_subtract_fusion) | copy-start | bytes 184
  51.0 2.6 collective-permute-start.2
  52.3 3.1 %collective-permute-start.3 = (f32[1,1920]{1,0:T(1,128)S(1)}, f32[1,1920]{1,0:T(1,128)S(1)}, u32[]{:S(2)}, u32[]{:S(2)}) collective-permute-start(f32[1,1920]{1,0:T(1,128)S(1)} %get-tuple-element.243), channel_id=1, source_target_pairs={{1,0},{2,1},{3,2},{4,3},{5,4},{6,5},{7,6},{8,7},{9,8},{10,9},{11,1... | collective-permute-start | bytes 23048 | tf_op jit(solution)/shard_map/ppermute | solution.py:26
  55.5 8.1 %collective-permute-start.4 = (f32[1,1920]{1,0:T(1,128)S(1)}, f32[1,1920]{1,0:T(1,128)S(1)}, u32[]{:S(2)}, u32[]{:S(2)}) collective-permute-start(f32[1,1920]{1,0:T(1,128)S(1)} %get-tuple-element.251), channel_id=1, source_target_pairs={{0,1},{1,2},{2,3},{3,4},{4,5},{5,6},{6,7},{7,8},{8,9},{9,10},{10,1... | collective-permute-start | bytes 23048 | tf_op jit(solution)/shard_map/ppermute | solution.py:23
  59.3 4.3 %collective-permute-start.5 = (f32[1,1920]{1,0:T(1,128)S(1)}, f32[1,1920]{1,0:T(1,128)S(1)}, u32[]{:S(2)}, u32[]{:S(2)}) collective-permute-start(f32[1,1920]{1,0:T(1,128)S(1)} %get-tuple-element.252), channel_id=1, source_target_pairs={{1,0},{2,1},{3,2},{4,3},{5,4},{6,5},{7,6},{8,7},{9,8},{10,9},{11,1... | collective-permute-start | bytes 23048 | tf_op jit(solution)/shard_map/ppermute | solution.py:26
  64.9 7.8 %collective-permute-start.6 = (f32[8,1,4,1920]{3,0,2,1:T(8,128)S(1)}, f32[8,1,4,1920]{3,0,2,1:T(8,128)S(1)}, u32[]{:S(2)}, u32[]{:S(2)}) collective-permute-start(f32[8,1,4,1920]{3,0,2,1:T(8,128)S(1)} %get-tuple-element.227), channel_id=1, source_target_pairs={{1,0},{2,1},{3,2},{4,3},{5,4},{6,5},{7,6},{8,7},{9,8},{10,9},{11,1... | collective-permute-start | bytes 737288 | tf_op jit(solution)/shard_map/ppermute | solution.py:26
  66.2 6.5 %collective-permute-start.7 = (f32[8,1,4,1920]{3,0,2,1:T(8,128)S(1)}, f32[8,1,4,1920]{3,0,2,1:T(8,128)S(1)}, u32[]{:S(2)}, u32[]{:S(2)}) collective-permute-start(f32[8,1,4,1920]{3,0,2,1:T(8,128)S(1)} %get-tuple-element.228), channel_id=1, source_target_pairs={{0,1},{1,2},{2,3},{3,4},{4,5},{5,6},{6,7},{7,8},{8,9},{9,10},{10,1... | collective-permute-start | bytes 737288 | tf_op jit(solution)/shard_map/ppermute | solution.py:23
  77.2 19.3 %copy-start.15 = (f32[2,1,80,128]{3,2,1,0:T(8,128)S(1)}, f32[2,1,80,128]{3,2,1,0:T(8,128)}, u32[]{:S(2)}) copy-start(f32[2,1,80,128]{3,2,1,0:T(8,128)} %param.55) | copy-start | bytes 245764
  77.4 19.4 %copy-start.9 = (f32[80,128]{1,0:T(8,128)S(1)}, f32[80,128]{1,0:T(8,128)}, u32[]{:S(2)}) copy-start(f32[80,128]{1,0:T(8,128)} %get-tuple-element.235) | copy-start | bytes 122884
  96.8 12.3 %copy-start.22 = (f32[75]{0:T(128)S(1)}, f32[75]{0:T(128)}, u32[]{:S(2)}) copy-start(f32[75]{0:T(128)} %copy-done.21) | copy-start | bytes 904
  96.9 12.3 %copy-start.25 = (s32[75]{0:T(128)S(1)}, s32[75]{0:T(128)}, u32[]{:S(2)}) copy-start(s32[75]{0:T(128)} %copy-done.24) | copy-start | bytes 904
  111.3 14.2 %copy-start.30 = (s32[15]{0:T(128)S(1)}, s32[15]{0:T(128)}, u32[]{:S(2)}) copy-start(s32[15]{0:T(128)} %copy-done.29) | copy-start | bytes 184
  112.3 2.6 collective-permute-start.8
  113.6 3.1 %collective-permute-start.9 = (f32[1,1920]{1,0:T(1,128)S(1)}, f32[1,1920]{1,0:T(1,128)S(1)}, u32[]{:S(2)}, u32[]{:S(2)}) collective-permute-start(f32[1,1920]{1,0:T(1,128)S(1)} %get-tuple-element.241), channel_id=1, source_target_pairs={{1,0},{2,1},{3,2},{4,3},{5,4},{6,5},{7,6},{8,7},{9,8},{10,9},{11,1... | collective-permute-start | bytes 23048 | tf_op jit(solution)/shard_map/ppermute | solution.py:26
  116.8 8.4 %collective-permute-start.10 = (f32[1,1920]{1,0:T(1,128)S(1)}, f32[1,1920]{1,0:T(1,128)S(1)}, u32[]{:S(2)}, u32[]{:S(2)}) collective-permute-start(f32[1,1920]{1,0:T(1,128)S(1)} %get-tuple-element.249), channel_id=1, source_target_pairs={{0,1},{1,2},{2,3},{3,4},{4,5},{5,6},{6,7},{7,8},{8,9},{9,10},{10,1... | collective-permute-start | bytes 23048 | tf_op jit(solution)/shard_map/ppermute | solution.py:23
  120.6 4.6 %collective-permute-start.11 = (f32[1,1920]{1,0:T(1,128)S(1)}, f32[1,1920]{1,0:T(1,128)S(1)}, u32[]{:S(2)}, u32[]{:S(2)}) collective-permute-start(f32[1,1920]{1,0:T(1,128)S(1)} %get-tuple-element.250), channel_id=1, source_target_pairs={{1,0},{2,1},{3,2},{4,3},{5,4},{6,5},{7,6},{8,7},{9,8},{10,9},{11,1... | collective-permute-start | bytes 23048 | tf_op jit(solution)/shard_map/ppermute | solution.py:26
  130.4 4.4 %collective-permute-start.12 = (f32[1,1920]{1,0:T(1,128)S(1)}, f32[1,1920]{1,0:T(1,128)S(1)}, u32[]{:S(2)}, u32[]{:S(2)}) collective-permute-start(f32[1,1920]{1,0:T(1,128)S(1)} %get-tuple-element.240), channel_id=1, source_target_pairs={{0,1},{1,2},{2,3},{3,4},{4,5},{5,6},{6,7},{7,8},{8,9},{9,10},{10,1... | collective-permute-start | bytes 23048 | tf_op jit(solution)/shard_map/ppermute | solution.py:23
  133.5 4.5 %collective-permute-start.13 = (f32[1,1920]{1,0:T(1,128)S(1)}, f32[1,1920]{1,0:T(1,128)S(1)}, u32[]{:S(2)}, u32[]{:S(2)}) collective-permute-start(f32[1,1920]{1,0:T(1,128)S(1)} %get-tuple-element.239), channel_id=1, source_target_pairs={{1,0},{2,1},{3,2},{4,3},{5,4},{6,5},{7,6},{8,7},{9,8},{10,9},{11,1... | collective-permute-start | bytes 23048 | tf_op jit(solution)/shard_map/ppermute | solution.py:26
  138.1 5.6 %collective-permute-start.14 = (f32[1,1920]{1,0:T(1,128)S(1)}, f32[1,1920]{1,0:T(1,128)S(1)}, u32[]{:S(2)}, u32[]{:S(2)}) collective-permute-start(f32[1,1920]{1,0:T(1,128)S(1)} %get-tuple-element.247), channel_id=1, source_target_pairs={{0,1},{1,2},{2,3},{3,4},{4,5},{5,6},{6,7},{7,8},{8,9},{9,10},{10,1... | collective-permute-start | bytes 23048 | tf_op jit(solution)/shard_map/ppermute | solution.py:23
  142.5 3.1 %collective-permute-start.15 = (f32[1,1920]{1,0:T(1,128)S(1)}, f32[1,1920]{1,0:T(1,128)S(1)}, u32[]{:S(2)}, u32[]{:S(2)}) collective-permute-start(f32[1,1920]{1,0:T(1,128)S(1)} %get-tuple-element.248), channel_id=1, source_target_pairs={{1,0},{2,1},{3,2},{4,3},{5,4},{6,5},{7,6},{8,7},{9,8},{10,9},{11,1... | collective-permute-start | bytes 23048 | tf_op jit(solution)/shard_map/ppermute | solution.py:26
  186.2 6.8 %collective-permute-start.16 = (f32[8,1,4,1920]{3,0,2,1:T(8,128)S(1)}, f32[8,1,4,1920]{3,0,2,1:T(8,128)S(1)}, u32[]{:S(2)}, u32[]{:S(2)}) collective-permute-start(f32[8,1,4,1920]{3,0,2,1:T(8,128)S(1)} %get-tuple-element.221), channel_id=1, source_target_pairs={{1,0},{2,1},{3,2},{4,3},{5,4},{6,5},{7,6},{8,7},{9,8},{10,9},{11,1... | collective-permute-start | bytes 737288 | tf_op jit(solution)/shard_map/ppermute | solution.py:26
  187.5 5.5 %collective-permute-start.17 = (f32[8,1,4,1920]{3,0,2,1:T(8,128)S(1)}, f32[8,1,4,1920]{3,0,2,1:T(8,128)S(1)}, u32[]{:S(2)}, u32[]{:S(2)}) collective-permute-start(f32[8,1,4,1920]{3,0,2,1:T(8,128)S(1)} %get-tuple-element.222), channel_id=1, source_target_pairs={{0,1},{1,2},{2,3},{3,4},{4,5},{5,6},{6,7},{7,8},{8,9},{9,10},{10,1... | collective-permute-start | bytes 737288 | tf_op jit(solution)/shard_map/ppermute | solution.py:23
  193.8 17.9 %copy-start.31 = (s32[15]{0:T(128)S(1)}, s32[15]{0:T(128)}, u32[]{:S(2)}) copy-start(s32[15]{0:T(128)} %copy-done.29) | copy-start | bytes 184
  194.9 5.2 %collective-permute-start.18 = (f32[1,1920]{1,0:T(1,128)S(1)}, f32[1,1920]{1,0:T(1,128)S(1)}, u32[]{:S(2)}, u32[]{:S(2)}) collective-permute-start(f32[1,1920]{1,0:T(1,128)S(1)} %get-tuple-element.238), channel_id=1, source_target_pairs={{0,1},{1,2},{2,3},{3,4},{4,5},{5,6},{6,7},{7,8},{8,9},{9,10},{10,1... | collective-permute-start | bytes 23048 | tf_op jit(solution)/shard_map/ppermute | solution.py:23
  198.8 5.1 %collective-permute-start.19 = (f32[1,1920]{1,0:T(1,128)S(1)}, f32[1,1920]{1,0:T(1,128)S(1)}, u32[]{:S(2)}, u32[]{:S(2)}) collective-permute-start(f32[1,1920]{1,0:T(1,128)S(1)} %get-tuple-element.237), channel_id=1, source_target_pairs={{1,0},{2,1},{3,2},{4,3},{5,4},{6,5},{7,6},{8,7},{9,8},{10,9},{11,1... | collective-permute-start | bytes 23048 | tf_op jit(solution)/shard_map/ppermute | solution.py:26
  204.0 5.6 %collective-permute-start.20 = (f32[1,1920]{1,0:T(1,128)S(1)}, f32[1,1920]{1,0:T(1,128)S(1)}, u32[]{:S(2)}, u32[]{:S(2)}) collective-permute-start(f32[1,1920]{1,0:T(1,128)S(1)} %get-tuple-element.245), channel_id=1, source_target_pairs={{0,1},{1,2},{2,3},{3,4},{4,5},{5,6},{6,7},{7,8},{8,9},{9,10},{10,1... | collective-permute-start | bytes 23048 | tf_op jit(solution)/shard_map/ppermute | solution.py:23
  208.3 3.1 %collective-permute-start.21 = (f32[1,1920]{1,0:T(1,128)S(1)}, f32[1,1920]{1,0:T(1,128)S(1)}, u32[]{:S(2)}, u32[]{:S(2)}) collective-permute-start(f32[1,1920]{1,0:T(1,128)S(1)} %get-tuple-element.246), channel_id=1, source_target_pairs={{1,0},{2,1},{3,2},{4,3},{5,4},{6,5},{7,6},{8,7},{9,8},{10,9},{11,1... | collective-permute-start | bytes 23048 | tf_op jit(solution)/shard_map/ppermute | solution.py:26
  212.7 16.4 %copy-start.8 = (f32[80,128]{1,0:T(8,128)S(1)}, f32[80,128]{1,0:T(8,128)}, u32[]{:S(2)}) copy-start(f32[80,128]{1,0:T(8,128)} %copy-done.7) | copy-start | bytes 122884
  230.7 12.0 %all-to-all-start.7 = ((f32[16,5,4,128]{3,2,1,0:T(4,128)}), f32[16,5,4,128]{3,2,1,0:T(4,128)S(1)}, u32[]{:S(2)}, u32[]{:S(2)}) async-start(f32[16,5,4,128]{3,2,1,0:T(4,128)} %bitcast.73), calls=%async_computation.7 | async-start | bytes 327680 | tf_op jit(solution)/shard_map/all_to_all | solution.py:115
  249.0 7.0 %collective-permute-start.22 = (f32[8,1,4,1920]{3,0,2,1:T(8,128)S(1)}, f32[8,1,4,1920]{3,0,2,1:T(8,128)S(1)}, u32[]{:S(2)}, u32[]{:S(2)}) collective-permute-start(f32[8,1,4,1920]{3,0,2,1:T(8,128)S(1)} %get-tuple-element.207), channel_id=1, source_target_pairs={{1,0},{2,1},{3,2},{4,3},{5,4},{6,5},{7,6},{8,7},{9,8},{10,9},{11,1... | collective-permute-start | bytes 737288 | tf_op jit(solution)/shard_map/ppermute | solution.py:26
  250.3 5.7 %collective-permute-start.23 = (f32[8,1,4,1920]{3,0,2,1:T(8,128)S(1)}, f32[8,1,4,1920]{3,0,2,1:T(8,128)S(1)}, u32[]{:S(2)}, u32[]{:S(2)}) collective-permute-start(f32[8,1,4,1920]{3,0,2,1:T(8,128)S(1)} %get-tuple-element.208), channel_id=1, source_target_pairs={{0,1},{1,2},{2,3},{3,4},{4,5},{5,6},{6,7},{7,8},{8,9},{9,10},{10,1... | collective-permute-start | bytes 737288 | tf_op jit(solution)/shard_map/ppermute | solution.py:23
  (22 other events, 141.8 us)
where the time goes:
time: 297 us; the launch traced here: 296 us
  blocking collectives  105 us (35%)
  starting transfers between devices  69.8 us (24%)
  local copies, waits for them, and re-layouts  39.4 us (13%)
  waiting for transfers between devices  36.9 us (12%)
  other arithmetic  20.9 us (7%)
  matrix products  19.6 us (7%)
  between operations  4.16 us (1%)
    all_to_all x3, blocking collectives, owner_round(): lax.all_to_all(outgoing, 'horiz', split_axis=0, concat_axis=0, tiled=True)  50.8 us
    ppermute x12, starting transfers between devices, with_halo(): lax.ppermute(lax.slice_in_dim(block, block.shape[dim] - width, None, axis...  39.3 us
    psum x1, blocking collectives, body(): lax.psum((jnp.sum(perturbation * perturbation), jnp.sum(perturbation * ad...  31.9 us
    all_to_all x2, blocking collectives, owner_round(): lax.all_to_all(result, 'horiz', split_axis=0, concat_axis=0, tiled=True)  22.1 us
    ppermute x12, starting transfers between devices, with_halo(): lax.ppermute(lax.slice_in_dim(block, 0, width, axis=dim), axis, backward)  15.5 us
    all_to_all x2, waiting for transfers between devices, owner_round(): lax.all_to_all(result, 'horiz', split_axis=0, concat_axis=0, tiled=True)  15.5 us
    ppermute x12, waiting for transfers between devices, with_halo(): lax.ppermute(lax.slice_in_dim(block, 0, width, axis=dim), axis, backward)  13.6 us
    all_to_all x1, starting transfers between devices, owner_round(): lax.all_to_all(outgoing, 'horiz', split_axis=0, concat_axis=0, tiled=True)  7.93 us
  transfers between devices with their start and end apart: 27, of which 9 were waited for; matrix products, arithmetic and copies ran while one was open for 7% of the time, Pallas kernels for 0%

commit v1 on v0

v1 whole, which is shorter than its diff:
```python
import functools

import jax
import jax.numpy as jnp
from jax import lax
from jax.experimental import pallas as pl
from jax.experimental.pallas import tpu as pltpu
from jax.sharding import PartitionSpec as P

LAT_DEV = 2
PAD = 8

KAPPA_V = 0.1
TIME_STEP = 0.3
FLUX_RATE = 0.05
FEEDBACK = 0.5
ASCENT = 0.5
EPSILON = 1e-06
HIGHEST = lax.Precision.HIGHEST
VMEM_BYTES = 48 * 1024 * 1024


def dot(a, b):
    return jnp.dot(a, b, precision=HIGHEST, preferred_element_type=jnp.float32)


def peer(me, offset, count):
    return lax.rem(me + offset + count, count)


def greet(count):
    me = lax.axis_index("horiz")
    barrier = pltpu.get_barrier_semaphore()

    def signal(offset, carry):
        pl.semaphore_signal(
            barrier, inc=1, device_id={"horiz": peer(me, offset, count)},
            device_id_type=pl.DeviceIdType.MESH,
        )
        return carry

    lax.fori_loop(1, count, signal, 0)
    pl.semaphore_wait(barrier, count - 1)


def block_copy(count, source, target, send, recv, offset):
    me = lax.axis_index("horiz")
    to = peer(me, offset, count)
    return pltpu.make_async_remote_copy(
        src_ref=source.at[to],
        dst_ref=target.at[me],
        send_sem=send.at[offset],
        recv_sem=recv.at[offset],
        device_id={"horiz": to},
        device_id_type=pl.DeviceIdType.MESH,
    )


def exchange(count, source, target, send, recv):
    me = lax.axis_index("horiz")

    def start(offset, carry):
        block_copy(count, source, target, send, recv, offset).start()
        return carry

    def finish(offset, carry):
        block_copy(count, source, target, send, recv, offset).wait()
        return carry

    lax.fori_loop(1, count, start, 0)
    target[me] = source[me]
    lax.fori_loop(1, count, finish, 0)


def shift_copy(count, source, target, sems, at, step):
    me = lax.axis_index("horiz")
    return pltpu.make_async_remote_copy(
        src_ref=source,
        dst_ref=target,
        send_sem=sems.at[at],
        recv_sem=sems.at[at + 1],
        device_id={"horiz": peer(me, step, count)},
        device_id_type=pl.DeviceIdType.MESH,
    )


def remap_sums(count, tiles, mat, sums, got_low, got_high, sems, at):
    me = lax.axis_index("horiz")
    half = sums.shape[0] // 2
    sums[...] = dot(mat[...], tiles[:, 0:128])
    down = shift_copy(count, sums.at[pl.ds(0, half)], got_high, sems, at, -1)
    up = shift_copy(count, sums.at[pl.ds(half, half)], got_low, sems, at + 2, 1)
    down.start()
    up.start()
    down.wait()
    up.wait()
    low = jnp.where(me > 0, got_low[...], 0.0)
    high = jnp.where(me < count - 1, got_high[...], 0.0)
    return jnp.concatenate([sums[0:half] + low, sums[half:] + high], axis=0)


def forward_kernel(
    count, halo, tiles_in, edge_low, edge_high, select, select_t, mat, mat_t, mix, air, wind,
    coupler, tiles, atmos, mixed_out, force_out, halo_low, halo_high, tile_low, tile_high,
    out_buf, in_buf, res_buf, back_buf, sums, got_low, got_high,
    send1, recv1, send2, recv2, sems,
):
    greet(count)
    if halo:
        rest_down = shift_copy(count, edge_low, halo_high, sems, 4, -1)
        rest_up = shift_copy(count, edge_high, halo_low, sems, 6, 1)
        rest_down.start()
        rest_up.start()
    out_buf[...] = dot(select[...], tiles_in[...]).reshape(out_buf.shape)
    exchange(count, out_buf, in_buf, send1, recv1)
    got = in_buf[...].reshape(mixed_out.shape)
    mixed = jnp.tanh(dot(mix[...], got))
    mixed_out[...] = mixed
    contrast = []
    for k in range(4):
        part = got[:, k * 128 : (k + 1) * 128]
        part = air[...] - part if k == 0 else part
        contrast.append(part + mixed[:, k * 128 : (k + 1) * 128])
    for c in range(4):
        force = jnp.tanh(sum(coupler[c, k] * contrast[k] for k in range(4)))
        force_out[:, c * 128 : (c + 1) * 128] = force
        flux = FLUX_RATE * wind[...] * force
        res_buf[:, :, c * 128 : (c + 1) * 128] = flux.reshape(res_buf.shape[:2] + (128,))
    exchange(count, res_buf, back_buf, send2, recv2)
    tiles[...] = tiles_in[...] + dot(select_t[...], back_buf[...].reshape(mixed_out.shape))
    total = jnp.tanh(remap_sums(count, tiles, mat, sums, got_low, got_high, sems, 0))
    atmos[...] = total
    tiles[:, 0:128] = tiles[:, 0:128] + FEEDBACK * dot(mat_t[...], total)
    if halo:
        finish_halo(count, tiles, tile_low, tile_high, sems)
        rest_down.wait()
        rest_up.wait()


def finish_halo(count, tiles, tile_low, tile_high, sems):
    head, tail = tile_high.shape[0], tile_low.shape[0]
    rows = tiles.shape[0]
    down = shift_copy(count, tiles.at[pl.ds(0, head)], tile_high, sems, 8, -1)
    up = shift_copy(count, tiles.at[pl.ds(rows - tail, tail)], tile_low, sems, 10, 1)
    down.start()
    up.start()
    down.wait()
    up.wait()


def adjoint_kernel(
    count, tiles_in, edge_low, edge_high, select, select_t, mat, mat_t, mix_t, wind,
    coupler, atmos, mixed, force, tiles, halo_low, halo_high, tile_low, tile_high,
    out_buf, in_buf, res_buf, back_buf, sums, got_low, got_high,
    send1, recv1, send2, recv2, sems,
):
    greet(count)
    rest_down = shift_copy(count, edge_low, halo_high, sems, 4, -1)
    rest_up = shift_copy(count, edge_high, halo_low, sems, 6, 1)
    tiles[...] = tiles_in[...]
    total = FEEDBACK * remap_sums(count, tiles, mat, sums, got_low, got_high, sems, 0)
    rest_down.start()
    rest_up.start()
    total = total * (1.0 - atmos[...] * atmos[...])
    tiles[:, 0:128] = tiles[:, 0:128] + dot(mat_t[...], total)
    out_buf[...] = dot(select[...], tiles[...]).reshape(out_buf.shape)
    exchange(count, out_buf, in_buf, send1, recv1)
    got = in_buf[...].reshape(mixed.shape)
    dforce = []
    for c in range(4):
        t = force[:, c * 128 : (c + 1) * 128]
        dforce.append(FLUX_RATE * wind[...] * (1.0 - t * t) * got[:, c * 128 : (c + 1) * 128])
    dcontrast = [sum(coupler[c, k] * dforce[c] for c in range(4)) for k in range(4)]
    joined = jnp.concatenate(dcontrast, axis=1)
    signed = jnp.concatenate([-dcontrast[0]] + dcontrast[1:], axis=1)
    held = mixed[...]
    result = signed + dot(mix_t[...], (1.0 - held * held) * joined)
    res_buf[...] = result.reshape(res_buf.shape)
    exchange(count, res_buf, back_buf, send2, recv2)
    tiles[...] = tiles[...] + dot(select_t[...], back_buf[...].reshape(mixed.shape))
    finish_halo(count, tiles, tile_low, tile_high, sems)
    rest_down.wait()
    rest_up.wait()


def sums_kernel(count, mine, total, own, got, send, recv):
    greet(count)
    me = lax.axis_index("horiz")

    def copy(offset):
        return pltpu.make_async_remote_copy(
            src_ref=mine,
            dst_ref=got.at[me],
            send_sem=send.at[offset],
            recv_sem=recv.at[offset],
            device_id={"horiz": peer(me, offset, count)},
            device_id_type=pl.DeviceIdType.MESH,
        )

    def start(offset, carry):
        copy(offset).start()
        return carry

    def finish(offset, carry):
        copy(offset).wait()
        return carry

    lax.fori_loop(1, count, start, 0)
    got[me] = mine[...]
    lax.fori_loop(1, count, finish, 0)
    total[...] = jnp.sum(got[...], axis=0)


def comm_call(kernel, outs, scratch, collective_id, smem_at=None, operands=()):
    specs = [
        pl.BlockSpec(memory_space=pltpu.SMEM if i == smem_at else pltpu.VMEM)
        for i in range(len(operands))
    ]
    return pl.pallas_call(
        kernel,
        out_shape=[jax.ShapeDtypeStruct(s, jnp.float32) for s in outs],
        in_specs=specs,
        out_specs=[pl.BlockSpec(memory_space=pltpu.VMEM)] * len(outs),
        scratch_shapes=scratch,
        compiler_params=pltpu.CompilerParams(
            collective_id=collective_id, has_side_effects=True, vmem_limit_bytes=VMEM_BYTES
        ),
    )(*operands)


def with_halo_permute(block):
    count = lax.axis_size("horiz")
    forward = [(i, i + 1) for i in range(count - 1)]
    backward = [(b, a) for a, b in forward]
    low = lax.ppermute(block[:, -1], "horiz", forward)
    high = lax.ppermute(block[:, 0], "horiz", backward)
    return low, high


def channel_mix_sum(mix, field):
    return jnp.einsum("lck,ljkx->ljcx", mix, field, precision=HIGHEST)


def level_diff(field):
    padded = jnp.pad(field, ((1, 1), (0, 0), (0, 0), (0, 0)))
    return padded[2:] + padded[:-2] - 2.0 * field


def horiz_lap(field, low, high):
    padded = jnp.concatenate([low[:, None], field, high[:, None]], axis=1)
    return (
        padded[:, 2:]
        + padded[:, :-2]
        + jnp.roll(field, -1, axis=3)
        + jnp.roll(field, 1, axis=3)
        - 4.0 * field
    )


def to_tiles(surface, tile_rows):
    row_count, channels, cells = surface.shape
    per_row = cells // 128
    pieces = surface.reshape(row_count, channels, per_row, 128).transpose(0, 2, 1, 3)
    flat = pieces.reshape(row_count * per_row, channels * 128)
    return jnp.pad(flat, ((0, tile_rows - flat.shape[0]), (0, 0)))


def from_tiles(tiles, row_count):
    per_row = tiles.shape[0] // row_count
    pieces = tiles.reshape(row_count, per_row, 4, 128).transpose(0, 2, 1, 3)
    return pieces.reshape(row_count, 4, per_row * 128)


def pad_slots(block, count, capacity, axis):
    shape = block.shape
    split = shape[:axis] + (count, capacity) + shape[axis + 1 :]
    widths = [(0, 0)] * len(split)
    widths[axis + 1] = (0, PAD - capacity)
    padded = jnp.pad(block.reshape(split), widths)
    return padded.reshape(shape[:axis] + (count * PAD,) + shape[axis + 1 :])


def body(
    perturbation,
    base_state,
    target_state,
    cost_weight,
    diffusivity,
    chan_mix,
    coupler_mix,
    owner_mix,
    air_temp,
    wind_speed,
    wet_list,
    wet_owner,
    remap_src,
    remap_tgt,
    remap_weight,
):
    count = lax.axis_size("horiz")
    me = lax.axis_index("horiz")
    levels, row_count, _, cells = base_state.shape
    capacity = air_temp.shape[2] // count
    tile_total = wet_list.shape[1]
    hour_count = air_temp.shape[0]
    per_row = cells // 128
    tile_rows = -(-tile_total // 8) * 8
    slots = count * PAD
    lat_pad = -(-per_row // 8) * 8
    lat_rows = (LAT_DEV + 2) * lat_pad

    owner = wet_owner[0]
    entry = jnp.arange(tile_total, dtype=jnp.int32)
    same = (owner[:, None] == owner[None, :]) & (entry[None, :] < entry[:, None])
    rank = jnp.sum(same.astype(jnp.int32), axis=1)
    slot = jnp.where(owner >= 0, owner * PAD + rank, -1)
    to_slot = (slot[None, :] == jnp.arange(slots, dtype=jnp.int32)[:, None]).astype(jnp.float32)
    of_tile = (wet_list[0][:, None] == jnp.arange(tile_rows, dtype=jnp.int32)[None, :]).astype(
        jnp.float32
    )
    select = dot(to_slot, of_tile)
    select_t = select.T

    src = remap_src - me * row_count
    tgt = remap_tgt - (me * LAT_DEV - 1)
    hit_src = (src[:, None] == jnp.arange(row_count, dtype=jnp.int32)[None, :]).astype(jnp.float32)
    hit_tgt = (tgt[:, None] == jnp.arange(LAT_DEV + 2, dtype=jnp.int32)[None, :]).astype(
        jnp.float32
    )
    small = jnp.sum(
        hit_tgt[:, :, None] * hit_src[:, None, :] * remap_weight[:, None, None], axis=0
    )
    eye = (
        jnp.arange(lat_pad, dtype=jnp.int32)[:, None]
        == jnp.arange(per_row, dtype=jnp.int32)[None, :]
    ).astype(jnp.float32)
    mat = (small[:, None, :, None] * eye[None, :, None, :]).reshape(lat_rows, row_count * per_row)
    mat = jnp.pad(mat, ((0, 0), (0, tile_rows - row_count * per_row)))
    mat_t = mat.T

    mix = pad_slots(pad_slots(owner_mix[0], count, capacity, 0), count, capacity, 1)
    mix_t = mix.T
    air = pad_slots(air_temp[:, 0], count, capacity, 1)
    wind = pad_slots(wind_speed[:, 0], count, capacity, 1)

    head = lat_pad
    tail = tile_rows - (row_count - 1) * per_row // 8 * 8
    tail_skip = (row_count - 1) * per_row - (tile_rows - tail)
    tile_shape = (tile_rows, 512)
    slot_shape = (slots, 512)
    lat_shape = (lat_rows, 128)
    edge_shape = (levels * 4, cells)
    halo_shapes = [edge_shape, edge_shape, (tail, 512), (head, 512)]
    scratch = (
        [pltpu.VMEM((count, PAD, 512), jnp.float32)] * 4
        + [pltpu.VMEM(lat_shape, jnp.float32)]
        + [pltpu.VMEM((lat_rows // 2, 128), jnp.float32)] * 2
        + [pltpu.SemaphoreType.DMA((count,))] * 4
        + [pltpu.SemaphoreType.DMA((12,))]
    )

    def edges(field):
        return field[:, 0].reshape(edge_shape), field[:, -1].reshape(edge_shape)

    def full_halo(low_rest, high_rest, low_tile, high_tile):
        low_top = from_tiles(low_tile[tail_skip : tail_skip + per_row], 1)[0]
        high_top = from_tiles(high_tile[:per_row], 1)[0]
        low = jnp.concatenate([low_top[None], low_rest.reshape(levels, 4, cells)[1:]], axis=0)
        high = jnp.concatenate([high_top[None], high_rest.reshape(levels, 4, cells)[1:]], axis=0)
        return jnp.where(me > 0, low, 0.0), jnp.where(me < count - 1, high, 0.0)

    def with_surface(field, tiles):
        top = from_tiles(tiles[:tile_total], row_count)
        return jnp.concatenate([top[None], field[1:]], axis=0)

    coeff = diffusivity[None, :, None, :]
    field = base_state + perturbation
    extra = jnp.broadcast_to(diffusivity[None, :, None, :], (1, row_count, 4, cells))
    low_all, high_all = with_halo_permute(jnp.concatenate([field, extra], axis=0))
    low, high = low_all[:levels], high_all[:levels]
    coeff_low, coeff_high = low_all[levels:], high_all[levels:]
    saved = []
    for hour in range(hour_count):
        drive = jnp.tanh(channel_mix_sum(chan_mix, field))
        field = (
            field
            + coeff * horiz_lap(field, low, high)
            + KAPPA_V * level_diff(field)
            + TIME_STEP * drive
        )
        edge_low, edge_high = edges(field)
        more = hour + 1 < hour_count
        outs = [tile_shape, lat_shape, slot_shape, slot_shape] + halo_shapes
        tiles, atmos, mixed, force, low_rest, high_rest, low_tile, high_tile = comm_call(
            functools.partial(forward_kernel, count, more),
            outs,
            scratch,
            0 if more else 1,
            smem_at=10,
            operands=(
                to_tiles(field[0], tile_rows), edge_low, edge_high, select, select_t, mat, mat_t,
                mix, air[hour], wind[hour], coupler_mix,
            ),
        )
        field = with_surface(field, tiles)
        if more:
            low, high = full_halo(low_rest, high_rest, low_tile, high_tile)
        saved.append((drive, atmos, mixed, force))
    adjoint = (cost_weight * cost_weight)[None, :, None, :] * (field - target_state)
    for hour in reversed(range(hour_count)):
        drive, atmos, mixed, force = saved[hour]
        edge_low, edge_high = edges(adjoint)
        tiles, low_rest, high_rest, low_tile, high_tile = comm_call(
            functools.partial(adjoint_kernel, count),
            [tile_shape] + halo_shapes,
            scratch,
            2,
            smem_at=9,
            operands=(
                to_tiles(adjoint[0], tile_rows), edge_low, edge_high, select, select_t, mat, mat_t,
                mix_t, wind[hour], coupler_mix, atmos, mixed, force,
            ),
        )
        adjoint = with_surface(adjoint, tiles)
        low, high = full_halo(low_rest, high_rest, low_tile, high_tile)
        adjoint = (
            adjoint
            + horiz_lap(coeff * adjoint, coeff_low * low, coeff_high * high)
            + KAPPA_V * level_diff(adjoint)
            + TIME_STEP
            * jnp.einsum(
                "lck,ljcx->ljkx", chan_mix, (1.0 - drive * drive) * adjoint, precision=HIGHEST
            )
        )
    cell_total = adjoint.size * count
    parts = [
        jnp.sum(perturbation * perturbation),
        jnp.sum(perturbation * adjoint),
        jnp.sum(adjoint * adjoint),
    ]
    row = jnp.arange(8, dtype=jnp.int32)[:, None]
    packed = jnp.broadcast_to(
        jnp.where(row == 0, parts[0], jnp.where(row == 1, parts[1], parts[2])), (8, 128)
    )
    (statistics,) = comm_call(
        functools.partial(sums_kernel, count),
        [(8, 128)],
        [
            pltpu.VMEM((8, 128), jnp.float32),
            pltpu.VMEM((count, 8, 128), jnp.float32),
            pltpu.SemaphoreType.DMA((count,)),
            pltpu.SemaphoreType.DMA((count,)),
        ],
        3,
        operands=(packed,),
    )
    mean_pp = statistics[0, 0] / cell_total
    mean_pg = statistics[1, 0] / cell_total
    mean_gg = statistics[2, 0] / cell_total
    grad_scale = lax.rsqrt(mean_gg + EPSILON)
    mean_sq = (
        mean_pp
        + 2.0 * ASCENT * grad_scale * mean_pg
        + ASCENT * ASCENT * grad_scale * grad_scale * mean_gg
    )
    stepped = perturbation + ASCENT * grad_scale * adjoint
    return stepped * lax.rsqrt(mean_sq + EPSILON)


def solution(mesh):
    placed = (
        P("member", "horiz", None, None),
        P(None, "horiz", None, None),
        P(None, "horiz", None, None),
        P("horiz", None),
        P("horiz", None),
        P(),
        P(),
        P("horiz", None, None),
        P(None, "horiz", None, None),
        P(None, "horiz", None, None),
        P("horiz", None),
        P("horiz", None),
        P("horiz"),
        P("horiz"),
        P("horiz"),
    )
    return jax.shard_map(
        body,
        mesh=mesh,
        in_specs=placed,
        out_specs=P("member", "horiz", None, None),
        check_vma=False,
    )
```

time: 297 us -> 206 us (0.69)
  Pallas kernels: 0 us -> 124 us
  blocking collectives: 105 us -> 0 us
  starting transfers between devices: 69.8 us -> 5.06 us
  waiting for transfers between devices: 36.9 us -> 0.01 us
  local copies, waits for them, and re-layouts: 39.4 us -> 20.9 us
  matrix products: 19.6 us -> 31.3 us
    pallas_call x0 -> x5, Pallas kernels: none -> 124 us  [comm_call(): pl.pallas_call(kernel, out_shape=[jax.ShapeDtypeStruct(s, jnp.float32) fo...]
    all_to_all x5 -> x0, blocking collectives: 72.9 us -> none  [the longest x3 50.8 us: owner_round(): lax.all_to_all(outgoing, 'horiz', split_axis=0, concat_axis=0, tiled=True)]
    ppermute x24 -> x2, starting transfers between devices: 54.8 us -> 5.06 us  [the longest x1 3.78 us: with_halo_permute(): low = lax.ppermute(block[:, -1], 'horiz', forward)]
    psum x1 -> x0, blocking collectives: 31.9 us -> none  [body(): lax.psum((jnp.sum(perturbation * perturbation), jnp.sum(perturbation * ad...]
    all_to_all x3 -> x0, waiting for transfers between devices: 23.3 us -> none  [the longest x2 15.5 us: owner_round(): lax.all_to_all(result, 'horiz', split_axis=0, concat_axis=0, tiled=True)]
    all_to_all x3 -> x0, starting transfers between devices: 15 us -> none  [the longest x1 7.93 us: owner_round(): lax.all_to_all(outgoing, 'horiz', split_axis=0, concat_axis=0, tiled=True)]
    scatter-add x16 -> x0, local copies, waits for them, and re-layouts: 14.9 us -> none  [the longest x2 6.07 us: body(): ocean_field = ocean_field.at[0].add(from_tiles(flux_tiles, row_count))]
    ppermute x24 -> x2, waiting for transfers between devices: 13.6 us -> 0.01 us  [the longest x1 0.01 us: with_halo_permute(): high = lax.ppermute(block[:, 0], 'horiz', backward)]
  transfers between devices with their start and end apart: 27 -> 2, of which waited for: 9 -> 0; matrix products, arithmetic and copies ran while one was open for 7% -> 3% of each run, Pallas kernels for 0% -> 0%
where the time goes in v1:
time: 206 us; the launch traced here: 205 us
  Pallas kernels  124 us (60%)
  matrix products  31.3 us (15%)
  local copies, waits for them, and re-layouts  20.9 us (10%)
  other arithmetic  20.7 us (10%)
  starting transfers between devices  5.06 us (2%)
  between operations  2.94 us (1%)
    pallas_call x5, Pallas kernels, comm_call(): pl.pallas_call(kernel, out_shape=[jax.ShapeDtypeStruct(s, jnp.float32) fo...  124 us
    dot_general x2, matrix products, body(): jnp.einsum('lck,ljcx->ljkx', chan_mix, (1.0 - drive * drive) * adjoint, p...  17.5 us
    dot_general x2, matrix products, channel_mix_sum(): return jnp.einsum('lck,ljkx->ljcx', mix, field, precision=HIGHEST)  13.5 us
    slice x6, local copies, waits for them, and re-layouts, horiz_lap(): jnp.roll(field, 1, axis=3)  7.46 us
    concatenate x3, other arithmetic, with_surface(): return jnp.concatenate([top[None], field[1:]], axis=0)  6.01 us
  transfers between devices with their start and end apart: 2, of which 0 were waited for; matrix products, arithmetic and copies ran while one was open for 3% of the time, Pallas kernels for 0%

profile of v1, /device:TPU:0, one launch (start us, length us, event | category | flops | bytes accessed | tf_op | source)
XLA Modules:
  0.0 205.1 jit_solution(9958231439036247647)
XLA Ops:
  0.0 2.0 add.133
  2.0 0.9 maximum_bitcast_fusion
  2.9 1.3 collective-permute-start
  4.2 3.8 %collective-permute-start.1 = (f32[9,4,1920]{2,1,0:T(4,128)}, f32[9,4,1920]{2,1,0:T(4,128)}, u32[]{:S(2)}, u32[]{:S(2)}) collective-permute-start(f32[9,4,1920]{2,1,0:T(4,128)} %get-tuple-element.53), channel_id=1, source_target_pairs={{0,1},{1,2},{2,3},{3,4},{4,5},{5,6},{6,7},{7,8},{8,9},{9,10},{10,1... | collective-permute-start | bytes 829448 | tf_op jit(solution)/shard_map/ppermute | solution.py:235
  8.1 2.2 %fusion.79 = (f32[8,5,4,1919]{3,2,1,0:T(4,128)}, f32[8,5,4,1919]{3,2,1,0:T(4,128)}) fusion(f32[8,5,4,1920]{3,2,1,0:T(4,128)S(1)} %add.133), kind=kLoop, calls=%fused_computation.153 | loop fusion | bytes 4912640 | tf_op jit(solution)/shard_map/jit(_roll_static)/slice | solution.py:255
  10.2 0.2 convert_reduce_fusion
  11.0 0.1 mul.274
  11.2 0.4 copy.113
  11.6 0.3 reshape_reshape.3
  12.0 0.2 copy-done.20
  12.2 0.3 fusion.60
  12.6 0.1 copy.103
  12.7 0.6 mul.253
  13.5 0.1 fusion.78
  13.6 1.0 slice_bitcast_fusion.1
  14.6 1.0 slice_bitcast_fusion
  15.6 6.5 %fusion.8 = (f32[8,5,4,1920]{3,2,1,0:T(4,128)S(1)}, f32[8,5,1920,4]{2,3,1,0:T(4,128)}) fusion(f32[8,5,4,1920]{3,2,1,0:T(4,128)S(1)} %add.133, f32[8,1,4,1920]{3,2,1,0:T(4,128)S(1)} %slice_bitcast_fusion, f32[8,1,4,1920]{3,2,1,0:T(4,128)S(1)} %slice_bitcast_fusion.1, f32[8,5,4,1]{3,2,1,0:T(4,128)S(1)} %get-tuple-element.79, ...), kind=kOutput, calls=%fused_computation.25 | convolution fusion | flops 20275200 | bytes 8104704 | tf_op jit(solution)/shard_map/lck,ljkx->ljcx/dot_general | solution.py:241
  22.1 1.1 slice.341
  23.7 0.3 copy-done
  23.9 31.7 %shard_map.145 = (f32[80,512]{1,0:T(8,128)S(1)}, f32[64,128]{1,0:T(8,128)S(1)}, f32[128,512]{1,0:T(8,128)S(1)}, f32[128,512]{1,0:T(8,128)S(1)}, f32[32,1920]{1,0...) custom-call(f32[80,512]{1,0:T(8,128)S(1)} %pad.46.tiles_in, ...), custom_call_target="tpu_custom_call" | custom-call | tf_op jit(solution)/shard_map/pallas_call | solution.py:219
  55.6 1.0 fusion.59
  56.7 2.6 %pad_maximum_fusion = f32[8,5,4,1920]{3,2,1,0:T(4,128)} fusion(f32[1,5,4,1920]{3,2,1,0:T(4,128)S(1)} %bitcast.153, f32[7,5,4,1920]{3,2,1,0:T(4,128)} %slice.341), kind=kLoop, calls=%fused_computation.4 | loop fusion | flops 307200 | bytes 2457600 | tf_op jit(solution)/shard_map/concatenate | solution.py:374
  59.3 2.4 %fusion.23 = (f32[8,5,4,1919]{3,2,1,0:T(4,128)}, f32[8,5,4,1919]{3,2,1,0:T(4,128)}) fusion(f32[1,5,4,1920]{3,2,1,0:T(4,128)S(1)} %bitcast.154, f32[7,5,4,1920]{3,2,1,0:T(4,128)S(1)} %copy-done.1), kind=kLoop, calls=%fused_computation.40 | loop fusion | flops 614080 | bytes 3685120 | tf_op jit(solution)/shard_map/concatenate | solution.py:374
  61.9 0.1 maximum_select_fusion
  62.0 7.0 %fusion.13 = (f32[8,5,4,1920]{3,2,1,0:T(4,128)S(1)}, f32[8,5,1920,4]{2,3,1,0:T(4,128)}) fusion(f32[8,5,4,1920]{3,2,1,0:T(4,128)} %pad_maximum_fusion, f32[8,1,4,1920]{3,2,1,0:T(4,128)S(1)} %get-tuple-element.97, f32[7,5,4,1920]{3,2,1,0:T(4,128)S(1)} %copy-done.1, f32[1,5,4,1920]{3,2,1,0:T(4,128)S(1)} %bitcast.155, ...), kind=kOutput, calls=%fused_computation.30 | convolution fusion | flops 21196800 | bytes 9317632 | tf_op jit(solution)/shard_map/lck,ljkx->ljcx/dot_general | solution.py:241
  69.6 26.4 %shard_map.146 = (f32[80,512]{1,0:T(8,128)S(1)}, f32[64,128]{1,0:T(8,128)S(1)}, f32[128,512]{1,0:T(8,128)S(1)}, f32[128,512]{1,0:T(8,128)S(1)}, f32[32,1920]{1,0...) custom-call(f32[80,512]{1,0:T(8,128)S(1)} %pad.53.tiles_in, ...), custom_call_target="tpu_custom_call" | custom-call | tf_op jit(solution)/shard_map/pallas_call | solution.py:219
  96.1 1.7 fusion.46
  97.9 1.1 slice.357
  99.4 29.9 %shard_map.147 = (f32[80,512]{1,0:T(8,128)S(1)}, f32[32,1920]{1,0:T(8,128)S(1)}, f32[32,1920]{1,0:T(8,128)S(1)}, f32[24,512]{1,0:T(8,128)S(1)}, f32[16,512]{1,0:T(8,128)S(1)}) custom-call(f32[80,512]{1,0:T(8,128)S(1)} %pad.54.tiles_in, f32[32,1920]{1,0:T(8,128)S(1)} %reshape_squeeze.55.edge_low, f32[32,1920]{1,0:T(8,128)S(1)} %reshape_squeeze.56.edge_high, ...), custom_call_target="tpu_custom_call" | custom-call | tf_op jit(solution)/shard_map/pallas_call | solution.py:219
  129.4 2.7 %broadcast_multiply_fusion.1 = (f32[8,5,4,1920]{3,2,1,0:T(4,128)S(1)}, f32[8,5,4,1920]{3,2,1,0:T(4,128)}) fusion(f32[5,1920]{1,0:T(8,128)S(1)} %copy-done.5, f32[7,5,4,1920]{3,2,1,0:T(4,128)} %slice.357, f32[1,5,4,1920]{3,2,1,0:T(4,128)S(1)} %bitcast.174), kind=kLoop, calls=%fused_computation.92 | loop fusion | flops 614400 | bytes 3724800 | tf_op jit(solution)/shard_map/mul | solution.py:428
  132.0 0.7 fusion.73
  132.8 2.2 %fusion.74 = (f32[8,5,4,1919]{3,2,1,0:T(4,128)}, f32[8,5,4,1919]{3,2,1,0:T(4,128)}) fusion(f32[8,5,4,1920]{3,2,1,0:T(4,128)S(1)} %get-tuple-element.66), kind=kLoop, calls=%fused_computation.148 | loop fusion | bytes 4912640 | tf_op jit(solution)/shard_map/jit(_roll_static)/slice | solution.py:255
  135.2 0.8 slice_bitcast_fusion.3
  136.0 0.8 slice_bitcast_fusion.2
  136.9 0.5 copy-done.7
  137.4 7.8 %fusion.1 = f32[8,5,4,1920]{3,2,1,0:T(4,128)S(1)} fusion(f32[8,4,4,1]{1,2,3,0:T(4,128)} %copy-done.13, f32[8,5,4,1920]{3,2,1,0:T(4,128)} %get-tuple-element.67, f32[8,5,4,1920]{3,2,1,0:T(4,128)S(1)} %get-tuple-element.66, f32[8,1,4,1920]{3,2,1,0:T(4,128)S(1)} %fusion.55, f32[8,1,4,1920]{3,2,1,0:T(4,128)S(1)} %fusion.54, ...), kind=kOutput, calls=%fused_computation.8 | convolution fusion | flops 20889600 | bytes 9273344 | tf_op jit(solution)/shard_map/lck,ljcx->ljkx/dot_general | solution.py:431
  145.2 1.0 copy-done.3
  146.6 29.4 %shard_map.148 = (f32[80,512]{1,0:T(8,128)S(1)}, f32[32,1920]{1,0:T(8,128)S(1)}, f32[32,1920]{1,0:T(8,128)S(1)}, f32[24,512]{1,0:T(8,128)S(1)}, f32[16,512]{1,0:T(8,128)S(1)}) custom-call(f32[80,512]{1,0:T(8,128)S(1)} %pad.56.tiles_in, f32[32,1920]{1,0:T(8,128)S(1)} %reshape_squeeze.58.edge_low, f32[32,1920]{1,0:T(8,128)S(1)} %reshape_squeeze.59.edge_high, ...), custom_call_target="tpu_custom_call" | custom-call | tf_op jit(solution)/shard_map/pallas_call | solution.py:219
  176.1 1.4 broadcast_multiply_fusion
  177.6 0.1 fusion.70
  177.7 2.2 %fusion.71 = (f32[8,5,4,1919]{3,2,1,0:T(4,128)}, f32[8,5,4,1919]{3,2,1,0:T(4,128)}) fusion(f32[8,5,4,1920]{3,2,1,0:T(4,128)S(1)} %get-tuple-element.58), kind=kLoop, calls=%fused_computation.145 | loop fusion | bytes 4912640 | tf_op jit(solution)/shard_map/jit(_roll_static)/slice | solution.py:255
  180.2 0.4 copy-done.8
  180.7 0.5 copy-done.2
  181.2 9.8 %multiply_reduce_fusion.2 = (f32[]{:T(128)}, f32[]{:T(128)}, f32[]{:T(128)}, f32[8,5,4,1920]{3,2,1,0:T(4,128)}) fusion(f32[8,5,4,1920]{3,2,1,0:T(4,128)S(1)} %copy-done.2, f32[8,4,4,1]{1,2,3,0:T(4,128)S(1)} %copy-done.14, f32[8,5,4,1920]{3,2,1,0:T(4,128)} %get-tuple-element.59, f32[8,5,1920,4]{2,3,1,0:T(4,128)} %get-tuple-element.92, ...), kind=kOutput, calls=%fused_computation.86 | convolution fusion | flops 22732796 | bytes 10323724 | tf_op jit(solution)/shard_map/lck,ljcx->ljkx/dot_general | solution.py:431
  191.0 1.9 compare_select_fusion.2
  193.0 6.9 %shard_map.149 = f32[8,128]{1,0:T(8,128)S(1)} custom-call(f32[8,128]{1,0:T(8,128)S(1)} %broadcast_in_dim.41.mine), custom_call_target="tpu_custom_call" | custom-call | tf_op jit(solution)/shard_map/pallas_call | solution.py:219
  199.9 0.6 fusion.80
  202.5 2.6 %add_multiply_fusion = f32[8,5,4,1920]{3,2,1,0:T(4,128)} fusion(f32[8,5,4,1920]{3,2,1,0:T(4,128)S(1)} %copy-done.2, f32[8,5,4,1920]{3,2,1,0:T(4,128)} %get-tuple-element.95, f32[]{:T(128)S(6)} %rsqrt.7, f32[]{:T(128)S(6)} %mul_shard_map.6), kind=kLoop, calls=%fused_computation.79 | loop fusion | flops 921600 | bytes 3686408 | tf_op jit(solution)/shard_map/mul | solution.py:467
  (128 shorter events, 3.9 us)
Async XLA Ops:
  0.0 2.0 copy-start.4
  2.9 10.7 %collective-permute-start = (f32[9,4,1920]{2,1,0:T(4,128)}, f32[9,4,1920]{2,1,0:T(4,128)}, u32[]{:S(2)}, u32[]{:S(2)}) collective-permute-start(f32[9,4,1920]{2,1,0:T(4,128)} %get-tuple-element.52), channel_id=1, source_target_pairs={{1,0},{2,1},{3,2},{4,3},{5,4},{6,5},{7,6},{8,7},{9,8},{10,9},{11,1... | collective-permute-start | bytes 829448 | tf_op jit(solution)/shard_map/ppermute | solution.py:236
  4.2 10.4 %collective-permute-start.1 = (f32[9,4,1920]{2,1,0:T(4,128)}, f32[9,4,1920]{2,1,0:T(4,128)}, u32[]{:S(2)}, u32[]{:S(2)}) collective-permute-start(f32[9,4,1920]{2,1,0:T(4,128)} %get-tuple-element.53), channel_id=1, source_target_pairs={{0,1},{1,2},{2,3},{3,4},{4,5},{5,6},{6,7},{7,8},{8,9},{9,10},{10,1... | collective-permute-start | bytes 829448 | tf_op jit(solution)/shard_map/ppermute | solution.py:235
  8.0 2.2 %copy-start.17 = (s32[1,75]{1,0:T(1,128)S(1)}, s32[1,75]{1,0:T(1,128)}, u32[]{:S(2)}) copy-start(s32[1,75]{1,0:T(1,128)} %param.26) | copy-start | bytes 904
  8.0 2.4 %copy-start.18 = (s32[15]{0:T(128)S(1)}, s32[15]{0:T(128)}, u32[]{:S(2)}) copy-start(s32[15]{0:T(128)} %param.28) | copy-start | bytes 184
  8.0 2.4 %copy-start.19 = (s32[15]{0:T(128)S(1)}, s32[15]{0:T(128)}, u32[]{:S(2)}) copy-start(s32[15]{0:T(128)} %param.27) | copy-start | bytes 184
  8.0 2.5 %copy-start.12 = (f32[1,80,80]{2,1,0:T(8,128)S(1)}, f32[1,80,80]{2,1,0:T(8,128)}, u32[]{:S(2)}) copy-start(f32[1,80,80]{2,1,0:T(8,128)} %param.22) | copy-start | bytes 76804
  8.1 2.5 %copy-start.10 = (f32[2,1,80,128]{3,2,1,0:T(8,128)S(1)}, f32[2,1,80,128]{3,2,1,0:T(8,128)}, u32[]{:S(2)}) copy-start(f32[2,1,80,128]{3,2,1,0:T(8,128)} %param.23) | copy-start | bytes 245764
  8.1 2.6 %copy-start.11 = (f32[2,1,80,128]{3,2,1,0:T(8,128)S(1)}, f32[2,1,80,128]{3,2,1,0:T(8,128)}, u32[]{:S(2)}) copy-start(f32[2,1,80,128]{3,2,1,0:T(8,128)} %param.24) | copy-start | bytes 245764
  8.1 2.8 %copy-start.16 = (f32[15]{0:T(128)S(1)}, f32[15]{0:T(128)}, u32[]{:S(2)}) copy-start(f32[15]{0:T(128)} %param.29) | copy-start | bytes 184
  11.5 0.7 copy-start.20
  11.5 1.0 copy-start.15
  11.6 1.1 copy-start.9
  12.7 9.4 %copy-start.13 = (f32[8,4,4,1]{1,2,3,0:T(4,128)}, f32[8,4,4,1]{1,2,3,0:T(4,128)S(1)}, u32[]{:S(2)}) copy-start(f32[8,4,4,1]{1,2,3,0:T(4,128)S(1)} %copy.103) | copy-start | bytes 1540
  23.2 0.7 copy-start
  56.7 2.6 %copy-start.1 = (f32[7,5,4,1920]{3,2,1,0:T(4,128)S(1)}, f32[7,5,4,1920]{3,2,1,0:T(4,128)}, u32[]{:S(2)}) copy-start(f32[7,5,4,1920]{3,2,1,0:T(4,128)} %slice.341) | copy-start | bytes 3225604
  99.3 30.0 %copy-start.5 = (f32[5,1920]{1,0:T(8,128)S(1)}, f32[5,1920]{1,0:T(8,128)}, u32[]{:S(2)}) copy-start(f32[5,1920]{1,0:T(8,128)} %param.19) | copy-start | bytes 115204
  136.8 0.6 copy-start.7
  145.2 1.0 copy-start.3
  146.5 29.6 %slice-start = ((f32[8,5,4,1920]{3,2,1,0:T(4,128)}), f32[7,5,4,1920]{3,2,1,0:T(4,128)S(1)}, s32[]{:S(2)}) async-start(f32[8,5,4,1920]{3,2,1,0:T(4,128)} %copy-done.3), calls=%async_computation | async-start | bytes 2150400 | tf_op jit(solution)/shard_map/slice | solution.py:374
  146.5 29.6 %copy-start.6 = (f32[5,1920]{1,0:T(8,128)S(1)}, f32[5,1920]{1,0:T(8,128)}, u32[]{:S(2)}) copy-start(f32[5,1920]{1,0:T(8,128)} %param.19) | copy-start | bytes 115204
  179.9 0.8 copy-start.8
  179.9 1.3 copy-start.2
  180.0 1.3 copy-start.14

commit v2 on v1

v2 whole, which is shorter than its diff:
```python
import functools

import jax
import jax.numpy as jnp
from jax import lax
from jax.experimental import pallas as pl
from jax.experimental.pallas import tpu as pltpu
from jax.sharding import PartitionSpec as P

LAT_DEV = 2
PAD = 8

KAPPA_V = 0.1
TIME_STEP = 0.3
FLUX_RATE = 0.05
FEEDBACK = 0.5
ASCENT = 0.5
EPSILON = 1e-06
HIGHEST = lax.Precision.HIGHEST
VMEM_BYTES = 48 * 1024 * 1024


def dot(a, b):
    return jnp.dot(a, b, precision=HIGHEST, preferred_element_type=jnp.float32)


def peer(me, offset, count):
    return lax.rem(me + offset + count, count)


def greet(count):
    me = lax.axis_index("horiz")
    barrier = pltpu.get_barrier_semaphore()

    def signal(offset, carry):
        pl.semaphore_signal(
            barrier, inc=1, device_id={"horiz": peer(me, offset, count)},
            device_id_type=pl.DeviceIdType.MESH,
        )
        return carry

    lax.fori_loop(1, count, signal, 0)
    pl.semaphore_wait(barrier, count - 1)


def block_copy(count, source, target, send, recv, offset):
    me = lax.axis_index("horiz")
    to = peer(me, offset, count)
    return pltpu.make_async_remote_copy(
        src_ref=source.at[to],
        dst_ref=target.at[me],
        send_sem=send.at[offset],
        recv_sem=recv.at[offset],
        device_id={"horiz": to},
        device_id_type=pl.DeviceIdType.MESH,
    )


def exchange(count, source, target, send, recv):
    me = lax.axis_index("horiz")

    def start(offset, carry):
        block_copy(count, source, target, send, recv, offset).start()
        return carry

    def finish(offset, carry):
        block_copy(count, source, target, send, recv, offset).wait()
        return carry

    lax.fori_loop(1, count, start, 0)
    target[me] = source[me]
    lax.fori_loop(1, count, finish, 0)


def shift_copy(count, source, target, sems, at, step):
    me = lax.axis_index("horiz")
    return pltpu.make_async_remote_copy(
        src_ref=source,
        dst_ref=target,
        send_sem=sems.at[at],
        recv_sem=sems.at[at + 1],
        device_id={"horiz": peer(me, step, count)},
        device_id_type=pl.DeviceIdType.MESH,
    )


def neighbours(field, low, high, width, group):
    rows = field.shape[0]
    tile = lax.rem(lax.broadcasted_iota(jnp.int32, field.shape, 0), group)
    lane = lax.broadcasted_iota(jnp.int32, field.shape, 1)
    east = pltpu.roll(field, 127, 1)
    following = jnp.where(
        tile == width - 1, pltpu.roll(east, width - 1, 0), pltpu.roll(east, rows - 1, 0)
    )
    east = jnp.where(lane == 127, following, east)
    west = pltpu.roll(field, 1, 1)
    before = jnp.where(tile == 0, pltpu.roll(west, rows - width + 1, 0), pltpu.roll(west, 1, 0))
    west = jnp.where(lane == 0, before, west)
    north = jnp.concatenate([low, field[: rows - group]], axis=0)
    south = jnp.concatenate([field[group:], high], axis=0)
    return north + south + east + west


def whole_kernel(
    count, width, group, hours, cell_total,
    pert, base, target, cost, coef, select, select_t, mat, mat_t, mix, mix_t, air, wind, chan,
    coupler, out,
    field_a, field_b, drive, halo_low, halo_high, coef_low, coef_high, out_buf, in_buf, mixed_s,
    force_s, atmos_s, sums, got_low, got_high, stat_src, stat_got,
    send, recv, near, stat_send, stat_recv,
):
    me = lax.axis_index("horiz")
    levels, _, rows, _ = pert.shape
    slots = mix.shape[0]
    half = sums.shape[0] // 2
    slot_shape = (slots, 512)
    used = [0, 0, 0]

    def near_copy(source, target_ref, step):
        at = used[0]
        used[0] += 2
        return shift_copy(count, source, target_ref, near, at, step)

    def pair(down_src, down_dst, up_src, up_dst):
        copies = [near_copy(down_src, down_dst, -1), near_copy(up_src, up_dst, 1)]
        for copy in copies:
            copy.start()
        return copies

    def finish(copies):
        for copy in copies:
            copy.wait()

    def halo(ref, at, first, number):
        here = pl.ds(first + 1, number)
        there = pl.ds(first, number)
        return pair(
            ref.at[here, :, pl.ds(0, group)],
            halo_high.at[at, there],
            ref.at[here, :, pl.ds(rows - group, group)],
            halo_low.at[at, there],
        )

    def swap(values):
        at = used[1]
        used[1] += 1
        out_buf[...] = values.reshape(out_buf.shape)
        exchange(count, out_buf, in_buf.at[at], send.at[at], recv.at[at])
        return in_buf[at].reshape(slot_shape)

    def surface(ref):
        return jnp.concatenate([ref[1, c] for c in range(4)], axis=1)

    def add_surface(ref, added):
        for c in range(4):
            ref[1, c] = ref[1, c] + added[:, c * 128 : (c + 1) * 128]

    def remap(ref):
        at = used[2]
        used[2] += 1
        sums[...] = dot(mat[...], ref[1, 0])
        finish(
            pair(
                sums.at[pl.ds(0, half)], got_high.at[at], sums.at[pl.ds(half, half)], got_low.at[at]
            )
        )
        low = jnp.where(me > 0, got_low[at], 0.0)
        high = jnp.where(me < count - 1, got_high[at], 0.0)
        return jnp.concatenate([sums[0:half] + low, sums[half:] + high], axis=0)

    def low_of(at, l, c):
        return jnp.where(me > 0, halo_low[at, l, c], 0.0)

    def high_of(at, l, c):
        return jnp.where(me < count - 1, halo_high[at, l, c], 0.0)

    zeros = jnp.zeros((4, rows, 128), jnp.float32)
    for ref in (field_a, field_b):
        ref[0] = zeros
        ref[levels + 1] = zeros

    def begin(l, total):
        mine = pert[l]
        field_a[l + 1] = base[l] + mine
        return total + jnp.sum(mine * mine, axis=0)

    pp = lax.fori_loop(0, levels, begin, jnp.zeros((rows, 128), jnp.float32))
    greet(count)
    waiting = halo(field_a, 0, 0, levels)
    waiting += pair(
        coef.at[pl.ds(0, group)], coef_high, coef.at[pl.ds(rows - group, group)], coef_low
    )

    def advance(hour, old, new):
        def level(l, carry):
            xs = [old[l + 1, c] for c in range(4)]
            for c in range(4):
                pushed = jnp.tanh(sum(chan[l * 16 + c * 4 + k] * xs[k] for k in range(4)))
                drive[hour, l, c] = pushed
                around = neighbours(xs[c], low_of(hour, l, c), high_of(hour, l, c), width, group)
                new[l + 1, c] = (
                    xs[c]
                    + coef[...] * (around - 4.0 * xs[c])
                    + KAPPA_V * (old[l, c] + old[l + 2, c] - 2.0 * xs[c])
                    + TIME_STEP * pushed
                )
            return carry

        lax.fori_loop(0, levels, level, 0)

    old, new = field_a, field_b
    for hour in range(hours):
        finish(waiting)
        advance(hour, old, new)
        more = hour + 1 < hours
        waiting = halo(new, hour + 1, 1, levels - 1) if more else []
        got = swap(dot(select[...], surface(new)))
        mixed = jnp.tanh(dot(mix[...], got))
        mixed_s[hour] = mixed
        contrast = []
        for k in range(4):
            part = got[:, k * 128 : (k + 1) * 128]
            part = air[hour] - part if k == 0 else part
            contrast.append(part + mixed[:, k * 128 : (k + 1) * 128])
        force = [
            jnp.tanh(sum(coupler[c, k] * contrast[k] for k in range(4))) for c in range(4)
        ]
        force_s[hour] = jnp.concatenate(force, axis=1)
        scaled = FLUX_RATE * wind[hour]
        back = swap(jnp.concatenate([scaled * f for f in force], axis=1))
        add_surface(new, dot(select_t[...], back))
        total = jnp.tanh(remap(new))
        atmos_s[hour] = total
        new[1, 0] = new[1, 0] + FEEDBACK * dot(mat_t[...], total)
        if more:
            waiting += halo(new, hour + 1, 0, 1)
        old, new = new, old

    def turn(l, carry):
        for c in range(4):
            new[l + 1, c] = cost[...] * cost[...] * (old[l + 1, c] - target[l, c])
        return carry

    lax.fori_loop(0, levels, turn, 0)
    old, new = new, old

    def retreat(hour, at, old, new, last):
        real = lax.rem(lax.broadcasted_iota(jnp.int32, (rows, 128), 0), group) < width
        factor = coef[...]

        def level(l, carry):
            pg, gg = carry
            adj = [old[l + 1, c] for c in range(4)]
            weighted = []
            for c in range(4):
                pushed = drive[hour, l, c]
                weighted.append((1.0 - pushed * pushed) * adj[c])
            for k in range(4):
                spread = factor * adj[k]
                around = neighbours(
                    spread, coef_low[...] * low_of(at, l, k), coef_high[...] * high_of(at, l, k),
                    width, group,
                )
                result = (
                    adj[k]
                    + jnp.where(real, around - 4.0 * spread, 0.0)
                    + KAPPA_V * (old[l, k] + old[l + 2, k] - 2.0 * adj[k])
                    + TIME_STEP * sum(chan[l * 16 + c * 4 + k] * weighted[c] for c in range(4))
                )
                new[l + 1, k] = result
                if last:
                    pg = pg + pert[l, k] * result
                    gg = gg + result * result
            return pg, gg

        start = jnp.zeros((rows, 128), jnp.float32)
        return lax.fori_loop(0, levels, level, (start, start))

    for hour in reversed(range(hours)):
        at = 2 * hours - 1 - hour
        total = FEEDBACK * remap(old)
        waiting = halo(old, at, 1, levels - 1)
        total = total * (1.0 - atmos_s[hour] * atmos_s[hour])
        old[1, 0] = old[1, 0] + dot(mat_t[...], total)
        got = swap(dot(select[...], surface(old)))
        scaled = FLUX_RATE * wind[hour]
        dforce = []
        for c in range(4):
            t = force_s[hour, :, c * 128 : (c + 1) * 128]
            dforce.append(scaled * (1.0 - t * t) * got[:, c * 128 : (c + 1) * 128])
        dcontrast = [sum(coupler[c, k] * dforce[c] for c in range(4)) for k in range(4)]
        joined = jnp.concatenate(dcontrast, axis=1)
        signed = jnp.concatenate([-dcontrast[0]] + dcontrast[1:], axis=1)
        held = mixed_s[hour]
        back = swap(signed + dot(mix_t[...], (1.0 - held * held) * joined))
        add_surface(old, dot(select_t[...], back))
        waiting += halo(old, at, 0, 1)
        finish(waiting)
        pg, gg = retreat(hour, at, old, new, hour == 0)
        old, new = new, old

    for i, value in enumerate((pp, pg, gg)):
        value = value if value.ndim == 2 else jnp.sum(value, axis=0)
        stat_src[i * 8 : (i + 1) * 8] = jnp.sum(value.reshape(rows // 8, 8, 128), axis=0)

    def stat_copy(offset):
        return pltpu.make_async_remote_copy(
            src_ref=stat_src,
            dst_ref=stat_got.at[me],
            send_sem=stat_send.at[offset],
            recv_sem=stat_recv.at[offset],
            device_id={"horiz": peer(me, offset, count)},
            device_id_type=pl.DeviceIdType.MESH,
        )

    def stat_start(offset, carry):
        stat_copy(offset).start()
        return carry

    def stat_finish(offset, carry):
        stat_copy(offset).wait()
        return carry

    lax.fori_loop(1, count, stat_start, 0)
    stat_got[me] = stat_src[...]
    lax.fori_loop(1, count, stat_finish, 0)
    stats = jnp.sum(stat_got[...], axis=0)
    mean_pp, mean_pg, mean_gg = [
        jnp.sum(stats[i * 8 : (i + 1) * 8], axis=(0, 1), keepdims=True) / cell_total
        for i in range(3)
    ]
    grad_scale = lax.rsqrt(mean_gg + EPSILON)
    mean_sq = (
        mean_pp
        + 2.0 * ASCENT * grad_scale * mean_pg
        + ASCENT * ASCENT * grad_scale * grad_scale * mean_gg
    )
    norm = lax.rsqrt(mean_sq + EPSILON)

    def close(l, carry):
        for c in range(4):
            out[l, c] = (pert[l, c] + ASCENT * grad_scale * old[l + 1, c]) * norm
        return carry

    lax.fori_loop(0, levels, close, 0)


def pad_slots(block, count, capacity, axis):
    shape = block.shape
    split = shape[:axis] + (count, capacity) + shape[axis + 1 :]
    widths = [(0, 0)] * len(split)
    widths[axis + 1] = (0, PAD - capacity)
    padded = jnp.pad(block.reshape(split), widths)
    return padded.reshape(shape[:axis] + (count * PAD,) + shape[axis + 1 :])


def body(
    perturbation,
    base_state,
    target_state,
    cost_weight,
    diffusivity,
    chan_mix,
    coupler_mix,
    owner_mix,
    air_temp,
    wind_speed,
    wet_list,
    wet_owner,
    remap_src,
    remap_tgt,
    remap_weight,
):
    count = lax.axis_size("horiz")
    me = lax.axis_index("horiz")
    levels, row_count, _, cells = base_state.shape
    capacity = air_temp.shape[2] // count
    tile_total = wet_list.shape[1]
    hour_count = air_temp.shape[0]
    width = cells // 128
    group = -(-width // 8) * 8
    rows = row_count * group
    slots = count * PAD
    lat_rows = (LAT_DEV + 2) * group

    owner = wet_owner[0]
    entry = jnp.arange(tile_total, dtype=jnp.int32)
    same = (owner[:, None] == owner[None, :]) & (entry[None, :] < entry[:, None])
    rank = jnp.sum(same.astype(jnp.int32), axis=1)
    slot = jnp.where(owner >= 0, owner * PAD + rank, -1)
    to_slot = (slot[None, :] == jnp.arange(slots, dtype=jnp.int32)[:, None]).astype(jnp.float32)
    place = jnp.where(owner >= 0, wet_list[0] // width * group + wet_list[0] % width, -1)
    of_tile = (place[:, None] == jnp.arange(rows, dtype=jnp.int32)[None, :]).astype(jnp.float32)
    select = dot(to_slot, of_tile)

    src = remap_src - me * row_count
    tgt = remap_tgt - (me * LAT_DEV - 1)
    hit_src = (src[:, None] == jnp.arange(row_count, dtype=jnp.int32)[None, :]).astype(jnp.float32)
    hit_tgt = (tgt[:, None] == jnp.arange(LAT_DEV + 2, dtype=jnp.int32)[None, :]).astype(
        jnp.float32
    )
    small = jnp.sum(
        hit_tgt[:, :, None] * hit_src[:, None, :] * remap_weight[:, None, None], axis=0
    )
    index = jnp.arange(group, dtype=jnp.int32)
    eye = (index[:, None] == index[None, :]).astype(jnp.float32)
    mat = (small[:, None, :, None] * eye[None, :, None, :]).reshape(lat_rows, rows)

    mix = pad_slots(pad_slots(owner_mix[0], count, capacity, 0), count, capacity, 1)
    air = pad_slots(air_temp[:, 0], count, capacity, 1)
    wind = pad_slots(wind_speed[:, 0], count, capacity, 1)

    def to_tiles(field):
        pieces = field.reshape(levels, row_count, 4, width, 128).transpose(0, 2, 1, 3, 4)
        widths = ((0, 0), (0, 0), (0, 0), (0, group - width), (0, 0))
        return jnp.pad(pieces, widths).reshape(levels, 4, rows, 128)

    def column_tiles(column):
        pieces = column.reshape(row_count, width, 128)
        return jnp.pad(pieces, ((0, 0), (0, group - width), (0, 0))).reshape(rows, 128)

    f32 = jnp.float32
    rounds = 2 * hour_count
    operands = (
        to_tiles(perturbation), to_tiles(base_state), to_tiles(target_state),
        column_tiles(cost_weight), column_tiles(diffusivity), select, select.T, mat, mat.T, mix,
        mix.T, air, wind, chan_mix.reshape(-1), coupler_mix,
    )
    specs = [pl.BlockSpec(memory_space=pltpu.VMEM)] * (len(operands) - 2)
    specs += [pl.BlockSpec(memory_space=pltpu.SMEM)] * 2
    result = pl.pallas_call(
        functools.partial(
            whole_kernel, count, width, group, hour_count, perturbation.size * count
        ),
        out_shape=jax.ShapeDtypeStruct((levels, 4, rows, 128), f32),
        in_specs=specs,
        out_specs=pl.BlockSpec(memory_space=pltpu.VMEM),
        scratch_shapes=[
            pltpu.VMEM((levels + 2, 4, rows, 128), f32),
            pltpu.VMEM((levels + 2, 4, rows, 128), f32),
            pltpu.VMEM((hour_count, levels, 4, rows, 128), f32),
            pltpu.VMEM((rounds, levels, 4, group, 128), f32),
            pltpu.VMEM((rounds, levels, 4, group, 128), f32),
            pltpu.VMEM((group, 128), f32),
            pltpu.VMEM((group, 128), f32),
            pltpu.VMEM((count, PAD, 512), f32),
            pltpu.VMEM((2 * rounds, count, PAD, 512), f32),
            pltpu.VMEM((hour_count, slots, 512), f32),
            pltpu.VMEM((hour_count, slots, 512), f32),
            pltpu.VMEM((hour_count, lat_rows, 128), f32),
            pltpu.VMEM((lat_rows, 128), f32),
            pltpu.VMEM((rounds, lat_rows // 2, 128), f32),
            pltpu.VMEM((rounds, lat_rows // 2, 128), f32),
            pltpu.VMEM((24, 128), f32),
            pltpu.VMEM((count, 24, 128), f32),
            pltpu.SemaphoreType.DMA((2 * rounds, count)),
            pltpu.SemaphoreType.DMA((2 * rounds, count)),
            pltpu.SemaphoreType.DMA((16 * rounds,)),
            pltpu.SemaphoreType.DMA((count,)),
            pltpu.SemaphoreType.DMA((count,)),
        ],
        compiler_params=pltpu.CompilerParams(
            collective_id=0, has_side_effects=True, vmem_limit_bytes=VMEM_BYTES
        ),
    )(*operands)
    pieces = result.reshape(levels, 4, row_count, group, 128)[:, :, :, :width]
    return pieces.transpose(0, 2, 1, 3, 4).reshape(perturbation.shape)


def solution(mesh):
    placed = (
        P("member", "horiz", None, None),
        P(None, "horiz", None, None),
        P(None, "horiz", None, None),
        P("horiz", None),
        P("horiz", None),
        P(),
        P(),
        P("horiz", None, None),
        P(None, "horiz", None, None),
        P(None, "horiz", None, None),
        P("horiz", None),
        P("horiz", None),
        P("horiz"),
        P("horiz"),
        P("horiz"),
    )
    return jax.shard_map(
        body,
        mesh=mesh,
        in_specs=placed,
        out_specs=P("member", "horiz", None, None),
        check_vma=False,
    )
```

time: 206 us -> 142 us (0.69)
  matrix products: 31.3 us -> 0.27 us
  other arithmetic: 20.7 us -> 4.42 us
  starting transfers between devices: 5.06 us -> 0 us
  local copies, waits for them, and re-layouts: 20.9 us -> 16.8 us
  Pallas kernels: 124 us -> 120 us
  between operations: 2.94 us -> 0.21 us
    dot_general x4 -> x0, matrix products: 31.1 us -> none  [the longest x2 17.5 us: body(): jnp.einsum('lck,ljcx->ljkx', chan_mix, (1.0 - drive * drive) * adjoint, p...]
    slice x31 -> x0, local copies, waits for them, and re-layouts: 10.8 us -> none  [the longest x6 7.46 us: horiz_lap(): jnp.roll(field, 1, axis=3)]
    mul x9 -> x0, other arithmetic: 9.37 us -> none  [the longest x2 4.08 us: body(): coeff * adjoint]
    reshape x10 -> x8, local copies, waits for them, and re-layouts: 0.31 us -> 8.7 us  [the longest x3 5.35 us: to_tiles(): field.reshape(levels, row_count, 4, width, 128).transpose(0, 2, 1, 3, 4)]
    concatenate x3 -> x0, other arithmetic: 6.01 us -> none  [with_surface(): return jnp.concatenate([top[None], field[1:]], axis=0)]
    ppermute x2 -> x0, starting transfers between devices: 5.06 us -> none  [the longest x1 3.78 us: with_halo_permute(): low = lax.ppermute(block[:, -1], 'horiz', forward)]
    pallas_call x5 -> x1, Pallas kernels: 124 us -> 120 us  [body(): pl.pallas_call(functools.partial(whole_kernel, count, width, group, hour_...]
    unnamed x55 -> x13, local copies, waits for them, and re-layouts: 3.84 us -> 6.1 us
  transfers between devices with their start and end apart: 2 -> 0, of which waited for: 0 -> 0; matrix products, arithmetic and copies ran while one was open for 3% -> 0% of each run, Pallas kernels for 0% -> 0%
where the time goes in v2:
time: 142 us
  Pallas kernels  120 us (85%)
  local copies, waits for them, and re-layouts  16.8 us (12%)
  other arithmetic  4.42 us (3%)
    pallas_call x1, Pallas kernels, body(): pl.pallas_call(functools.partial(whole_kernel, count, width, group, hour_...  120 us
    unnamed x13, local copies, waits for them, and re-layouts  6.1 us
    reshape x3, local copies, waits for them, and re-layouts, to_tiles(): field.reshape(levels, row_count, 4, width, 128).transpose(0, 2, 1, 3, 4)  5.35 us

profile of v2, /device:TPU:0, one launch (start us, length us, event | category | flops | bytes accessed | tf_op | source)
XLA Modules:
  0.0 141.8 jit_solution(981562894789715364)
XLA Ops:
  0.0 0.7 broadcast_subtract_fusion.1
  0.7 0.7 broadcast_subtract_fusion
  1.3 0.7 compare_select_fusion
  2.0 0.9 convert_reduce_fusion
  2.9 0.7 fusion.9
  3.6 0.7 multiply_reduce_fusion
  4.3 0.8 copy.53
  5.1 0.1 reshape.159.chan
  5.3 0.3 fusion
  5.5 0.9 reshape.152
  6.4 0.8 reshape.154
  7.3 0.1 copy.54.select
  7.4 0.8 reshape_squeeze.9
  8.1 0.9 copy.49
  9.1 0.9 copy.51
  10.1 0.1 broadcast_multiply_fusion
  10.2 0.1 mul.75
  10.3 0.1 copy.55.mat
  10.4 0.4 copy.66
  10.8 0.0 copy-start.1
  10.8 0.3 reshape_reshape.3
  11.2 0.1 copy.56.mix
  11.3 0.8 copy-done.1
  12.1 0.6 reshape.162
  12.7 0.1 copy.63
  12.8 0.1 pad.32.clone
  13.0 1.9 %reshape.163 = f32[8,5,4,15,128]{4,3,2,1,0:T(8,128)S(1)} reshape(f32[8,5,4,1920]{3,2,1,0:T(4,128)} %param.16) | data formatting | bytes 2457600 | tf_op jit(solution)/shard_map/reshape | solution.py:414
  14.9 0.1 copy.64
  15.0 0.1 pad.33.clone
  15.1 2.8 %reshape.164 = f32[8,5,4,15,128]{4,3,2,1,0:T(8,128)} reshape(f32[8,5,4,1920]{3,2,1,0:T(4,128)} %param.17) | data formatting | bytes 2457600 | tf_op jit(solution)/shard_map/reshape | solution.py:414
  18.0 1.4 copy.65
  19.4 0.0 copy-start
  19.4 0.1 pad.34.clone
  19.5 0.6 copy-done
  20.0 120.0 %shard_map.145 = f32[8,4,80,128]{3,2,1,0:T(8,128)S(1)} custom-call(f32[8,4,80,128]{3,2,1,0:T(8,128)S(1)} %bitcast.57, f32[8,4,80,128]{3,2,1,0:T(8,128)S(1)} %bitcast.58, f32[8,4,80,128]{3,2,1,0:T(8,128)S(1)} %bitcast.59, f32[80,128]{1,0:T(8,128)S(1)} %bitcast.61, f32[80,128]{1,0:T(8,128)S(1)} %bitcast.62, f32[128,80]{1,0:T(8,128)S(1)} %copy.54.select, ...), custom_call_target="tpu_custom_call" | custom-call | tf_op jit(solution)/shard_map/pallas_call | solution.py:431
  140.1 0.1 copy_bitcast_fusion
  140.2 0.2 reshape.161
  140.4 1.3 copy.58
  (10 shorter events, 0.1 us)
Async XLA Ops:
  10.8 1.3 copy-start.1
  19.4 0.7 copy-start

commit v3 on v2

--- a/solution.py
+++ b/solution.py
@@ -24,6 +24,12 @@
     return jnp.dot(a, b, precision=HIGHEST, preferred_element_type=jnp.float32)
 
 
+def dot_t(a, b):
+    return lax.dot_general(
+        a, b, (((0,), (0,)), ((), ())), precision=HIGHEST, preferred_element_type=jnp.float32
+    )
+
+
 def peer(me, offset, count):
     return lax.rem(me + offset + count, count)
 
@@ -40,15 +46,15 @@
         return carry
 
     lax.fori_loop(1, count, signal, 0)
-    pl.semaphore_wait(barrier, count - 1)
-
-
-def block_copy(count, source, target, send, recv, offset):
+    return lambda: pl.semaphore_wait(barrier, count - 1)
+
+
+def block_copy(count, capacity, source, target, send, recv, offset):
     me = lax.axis_index("horiz")
     to = peer(me, offset, count)
     return pltpu.make_async_remote_copy(
-        src_ref=source.at[to],
-        dst_ref=target.at[me],
+        src_ref=source.at[to, pl.ds(0, capacity)],
+        dst_ref=target.at[me, pl.ds(0, capacity)],
         send_sem=send.at[offset],
         recv_sem=recv.at[offset],
         device_id={"horiz": to},
@@ -56,15 +62,15 @@
     )
 
 
-def exchange(count, source, target, send, recv):
+def exchange(count, capacity, source, target, send, recv):
     me = lax.axis_index("horiz")
 
     def start(offset, carry):
-        block_copy(count, source, target, send, recv, offset).start()
+        block_copy(count, capacity, source, target, send, recv, offset).start()
         return carry
 
     def finish(offset, carry):
-        block_copy(count, source, target, send, recv, offset).wait()
+        block_copy(count, capacity, source, target, send, recv, offset).wait()
         return carry
 
     lax.fori_loop(1, count, start, 0)
@@ -103,15 +109,15 @@
 
 def whole_kernel(
     count, width, group, hours, cell_total,
-    pert, base, target, cost, coef, select, select_t, mat, mat_t, mix, mix_t, air, wind, chan,
-    coupler, out,
-    field_a, field_b, drive, halo_low, halo_high, coef_low, coef_high, out_buf, in_buf, mixed_s,
+    pert, base, target, cost, coef, select, mat, mix_in, air_in, wind_in, chan, coupler, out,
+    mix, air, wind, field_a, field_b, drive, halo_low, halo_high, coef_low, coef_high, out_buf, in_buf, mixed_s,
     force_s, atmos_s, sums, got_low, got_high, stat_src, stat_got,
     send, recv, near, stat_send, stat_recv,
 ):
     me = lax.axis_index("horiz")
     levels, _, rows, _ = pert.shape
     slots = mix.shape[0]
+    capacity = mix_in.shape[1] // count
     half = sums.shape[0] // 2
     slot_shape = (slots, 512)
     used = [0, 0, 0]
@@ -145,7 +151,7 @@
         at = used[1]
         used[1] += 1
         out_buf[...] = values.reshape(out_buf.shape)
-        exchange(count, out_buf, in_buf.at[at], send.at[at], recv.at[at])
+        exchange(count, capacity, out_buf, in_buf.at[at], send.at[at], recv.at[at])
         return in_buf[at].reshape(slot_shape)
 
     def surface(ref):
@@ -174,6 +180,9 @@
     def high_of(at, l, c):
         return jnp.where(me < count - 1, halo_high[at, l, c], 0.0)
 
+    for at in range(in_buf.shape[0]):
+        in_buf[at, :, capacity:] = jnp.zeros((count, PAD - capacity, 512), jnp.float32)
+    all_in = greet(count)
     zeros = jnp.zeros((4, rows, 128), jnp.float32)
     for ref in (field_a, field_b):
         ref[0] = zeros
@@ -185,11 +194,22 @@
         return total + jnp.sum(mine * mine, axis=0)
 
     pp = lax.fori_loop(0, levels, begin, jnp.zeros((rows, 128), jnp.float32))
-    greet(count)
+    all_in()
     waiting = halo(field_a, 0, 0, levels)
     waiting += pair(
         coef.at[pl.ds(0, group)], coef_high, coef.at[pl.ds(rows - group, group)], coef_low
     )
+    slot = lax.broadcasted_iota(jnp.int32, (slots, count * capacity), 0)
+    cell = lax.broadcasted_iota(jnp.int32, (slots, count * capacity), 1)
+    rank = slot % PAD
+    widen = ((slot // PAD * capacity + rank == cell) & (rank < capacity)).astype(jnp.float32)
+    mix[...] = lax.dot_general(
+        dot(widen, mix_in[0]), widen, (((1,), (1,)), ((), ())), precision=HIGHEST,
+        preferred_element_type=jnp.float32,
+    )
+    for hour in range(hours):
+        air[hour] = dot(widen, air_in[hour, 0])
+        wind[hour] = dot(widen, wind_in[hour, 0])
 
     def advance(hour, old, new):
         def level(l, carry):
@@ -228,10 +248,10 @@
         force_s[hour] = jnp.concatenate(force, axis=1)
         scaled = FLUX_RATE * wind[hour]
         back = swap(jnp.concatenate([scaled * f for f in force], axis=1))
-        add_surface(new, dot(select_t[...], back))
+        add_surface(new, dot_t(select[...], back))
         total = jnp.tanh(remap(new))
         atmos_s[hour] = total
-        new[1, 0] = new[1, 0] + FEEDBACK * dot(mat_t[...], total)
+        new[1, 0] = new[1, 0] + FEEDBACK * dot_t(mat[...], total)
         if more:
             waiting += halo(new, hour + 1, 0, 1)
         old, new = new, old
@@ -281,7 +301,7 @@
         total = FEEDBACK * remap(old)
         waiting = halo(old, at, 1, levels - 1)
         total = total * (1.0 - atmos_s[hour] * atmos_s[hour])
-        old[1, 0] = old[1, 0] + dot(mat_t[...], total)
+        old[1, 0] = old[1, 0] + dot_t(mat[...], total)
         got = swap(dot(select[...], surface(old)))
         scaled = FLUX_RATE * wind[hour]
         dforce = []
@@ -292,8 +312,8 @@
         joined = jnp.concatenate(dcontrast, axis=1)
         signed = jnp.concatenate([-dcontrast[0]] + dcontrast[1:], axis=1)
         held = mixed_s[hour]
-        back = swap(signed + dot(mix_t[...], (1.0 - held * held) * joined))
-        add_surface(old, dot(select_t[...], back))
+        back = swap(signed + dot_t(mix[...], (1.0 - held * held) * joined))
+        add_surface(old, dot_t(select[...], back))
         waiting += halo(old, at, 0, 1)
         finish(waiting)
         pg, gg = retreat(hour, at, old, new, hour == 0)
@@ -343,15 +363,6 @@
         return carry
 
     lax.fori_loop(0, levels, close, 0)
-
-
-def pad_slots(block, count, capacity, axis):
-    shape = block.shape
-    split = shape[:axis] + (count, capacity) + shape[axis + 1 :]
-    widths = [(0, 0)] * len(split)
-    widths[axis + 1] = (0, PAD - capacity)
-    padded = jnp.pad(block.reshape(split), widths)
-    return padded.reshape(shape[:axis] + (count * PAD,) + shape[axis + 1 :])
 
 
 def body(
@@ -374,7 +385,6 @@
     count = lax.axis_size("horiz")
     me = lax.axis_index("horiz")
     levels, row_count, _, cells = base_state.shape
-    capacity = air_temp.shape[2] // count
     tile_total = wet_list.shape[1]
     hour_count = air_temp.shape[0]
     width = cells // 128
@@ -406,10 +416,6 @@
     eye = (index[:, None] == index[None, :]).astype(jnp.float32)
     mat = (small[:, None, :, None] * eye[None, :, None, :]).reshape(lat_rows, rows)
 
-    mix = pad_slots(pad_slots(owner_mix[0], count, capacity, 0), count, capacity, 1)
-    air = pad_slots(air_temp[:, 0], count, capacity, 1)
-    wind = pad_slots(wind_speed[:, 0], count, capacity, 1)
-
     def to_tiles(field):
         pieces = field.reshape(levels, row_count, 4, width, 128).transpose(0, 2, 1, 3, 4)
         widths = ((0, 0), (0, 0), (0, 0), (0, group - width), (0, 0))
@@ -423,8 +429,8 @@
     rounds = 2 * hour_count
     operands = (
         to_tiles(perturbation), to_tiles(base_state), to_tiles(target_state),
-        column_tiles(cost_weight), column_tiles(diffusivity), select, select.T, mat, mat.T, mix,
-        mix.T, air, wind, chan_mix.reshape(-1), coupler_mix,
+        column_tiles(cost_weight), column_tiles(diffusivity), select, mat, owner_mix, air_temp,
+        wind_speed, chan_mix.reshape(-1), coupler_mix,
     )
     specs = [pl.BlockSpec(memory_space=pltpu.VMEM)] * (len(operands) - 2)
     specs += [pl.BlockSpec(memory_space=pltpu.SMEM)] * 2
@@ -436,6 +442,9 @@
         in_specs=specs,
         out_specs=pl.BlockSpec(memory_space=pltpu.VMEM),
         scratch_shapes=[
+            pltpu.VMEM((slots, slots), f32),
+            pltpu.VMEM((hour_count, slots, 128), f32),
+            pltpu.VMEM((hour_count, slots, 128), f32),
             pltpu.VMEM((levels + 2, 4, rows, 128), f32),
             pltpu.VMEM((levels + 2, 4, rows, 128), f32),
             pltpu.VMEM((hour_count, levels, 4, rows, 128), f32),

time: 142 us -> 128 us (0.901)
  Pallas kernels: 120 us -> 109 us
  local copies, waits for them, and re-layouts: 16.8 us -> 13.8 us
    pallas_call x1, Pallas kernels: 120 us -> 109 us  [body(): pl.pallas_call(functools.partial(whole_kernel, count, width, group, hour_...]
    unnamed x13 -> x12, local copies, waits for them, and re-layouts: 6.1 us -> 3.18 us
where the time goes in v3:
time: 128 us; the launch traced here: 127 us
  Pallas kernels  109 us (85%)
  local copies, waits for them, and re-layouts  13.8 us (11%)
  other arithmetic  4.42 us (3%)
    pallas_call x1, Pallas kernels, body(): pl.pallas_call(functools.partial(whole_kernel, count, width, group, hour_...  109 us
    reshape x3, local copies, waits for them, and re-layouts, to_tiles(): field.reshape(levels, row_count, 4, width, 128).transpose(0, 2, 1, 3, 4)  6.63 us
    unnamed x12, local copies, waits for them, and re-layouts  3.18 us

profile of v3, /device:TPU:0, one launch (start us, length us, event | category | flops | bytes accessed | tf_op | source)
XLA Modules:
  0.0 127.2 jit_solution(9906770018229045143)
XLA Ops:
  0.0 0.7 broadcast_subtract_fusion.1
  0.7 0.7 broadcast_subtract_fusion
  1.3 0.7 compare_select_fusion
  2.0 0.9 convert_reduce_fusion
  2.9 0.7 fusion.9
  3.6 0.7 multiply_reduce_fusion
  4.3 0.8 copy.39
  5.1 0.1 reshape.147.chan
  5.3 0.8 reshape.143
  6.1 0.8 reshape.145
  7.0 0.2 fusion.select
  7.2 0.1 broadcast_multiply_fusion
  7.3 0.1 mul.75
  7.4 0.1 copy.41.mat
  7.5 1.9 %reshape.150 = f32[8,5,4,15,128]{4,3,2,1,0:T(8,128)S(1)} reshape(f32[8,5,4,1920]{3,2,1,0:T(4,128)} %param.15) | data formatting | bytes 2457600 | tf_op jit(solution)/shard_map/reshape | solution.py:420
  9.4 0.1 copy.49
  9.5 0.1 pad.17.clone
  9.6 1.9 %reshape.151 = f32[8,5,4,15,128]{4,3,2,1,0:T(8,128)S(1)} reshape(f32[8,5,4,1920]{3,2,1,0:T(4,128)} %param.16) | data formatting | bytes 2457600 | tf_op jit(solution)/shard_map/reshape | solution.py:420
  11.5 0.1 copy.50
  11.6 0.1 pad.18.clone
  11.7 2.8 %reshape.152 = f32[8,5,4,15,128]{4,3,2,1,0:T(8,128)} reshape(f32[8,5,4,1920]{3,2,1,0:T(4,128)} %param.17) | data formatting | bytes 2457600 | tf_op jit(solution)/shard_map/reshape | solution.py:420
  14.5 1.4 %copy.51 = f32[8,4,5,15,128]{4,3,2,1,0:T(8,128)S(1)} copy(f32[8,4,5,15,128]{4,3,1,2,0:T(8,128)} %bitcast.49) | data formatting | bytes 2457600
  15.9 0.0 copy-start
  15.9 0.0 copy-start.1
  15.9 0.0 copy-start.2
  16.0 0.0 copy-start.3
  16.0 0.1 pad.19.clone
  16.1 0.7 copy-done
  16.8 0.0 copy-done.1
  16.9 0.0 copy-done.2
  16.9 0.0 copy-done.3
  16.9 108.7 %shard_map.145 = f32[8,4,80,128]{3,2,1,0:T(8,128)S(1)} custom-call(f32[8,4,80,128]{3,2,1,0:T(8,128)S(1)} %bitcast.42, f32[8,4,80,128]{3,2,1,0:T(8,128)S(1)} %bitcast.43, f32[8,4,80,128]{3,2,1,0:T(8,128)S(1)} %bitcast.44, f32[80,128]{1,0:T(8,128)S(1)} %bitcast.45, f32[80,128]{1,0:T(8,128)S(1)} %bitcast.46, f32[128,80]{1,0:T(8,128)S(1)} %fusion.select, ...), custom_call_target="tpu_custom_call" | custom-call | tf_op jit(solution)/shard_map/pallas_call | solution.py:437
  125.5 0.1 copy_bitcast_fusion
  125.7 0.2 reshape.149
  125.9 1.3 %copy.43 = f32[8,5,4,1920]{3,2,1,0:T(4,128)} copy(f32[8,5,4,1920]{3,0,2,1:T(8,128)S(1)} %reshape.149) | data formatting | bytes 2457600 | tf_op jit(solution)/shard_map/reshape | solution.py:476
  (5 shorter events, 0.0 us)
Async XLA Ops:
  15.9 0.9 copy-start
  15.9 0.9 copy-start.1
  15.9 0.9 copy-start.2
  16.0 0.9 copy-start.3

commit v4 on v3

--- a/solution.py
+++ b/solution.py
@@ -62,7 +62,7 @@
     )
 
 
-def exchange(count, capacity, source, target, send, recv):
+def exchange(count, capacity, source, target, send, recv, work):
     me = lax.axis_index("horiz")
 
     def start(offset, carry):
@@ -75,6 +75,7 @@
 
     lax.fori_loop(1, count, start, 0)
     target[me] = source[me]
+    work()
     lax.fori_loop(1, count, finish, 0)
 
 
@@ -109,7 +110,9 @@
 
 def whole_kernel(
     count, width, group, hours, cell_total,
-    pert, base, target, cost, coef, select, mat, mix_in, air_in, wind_in, chan, coupler, out,
+    pert, base, target, cost, coef, wet_list, wet_owner, mix_in, air_in, wind_in, chan, coupler,
+    remap_src, remap_tgt, remap_weight, out,
+    select, mat,
     mix, air, wind, field_a, field_b, drive, halo_low, halo_high, coef_low, coef_high, out_buf, in_buf, mixed_s,
     force_s, atmos_s, sums, got_low, got_high, stat_src, stat_got,
     send, recv, near, stat_send, stat_recv,
@@ -147,11 +150,11 @@
             halo_low.at[at, there],
         )
 
-    def swap(values):
+    def swap(values, work=lambda: None):
         at = used[1]
         used[1] += 1
         out_buf[...] = values.reshape(out_buf.shape)
-        exchange(count, capacity, out_buf, in_buf.at[at], send.at[at], recv.at[at])
+        exchange(count, capacity, out_buf, in_buf.at[at], send.at[at], recv.at[at], work)
         return in_buf[at].reshape(slot_shape)
 
     def surface(ref):
@@ -199,6 +202,33 @@
     waiting += pair(
         coef.at[pl.ds(0, group)], coef_high, coef.at[pl.ds(rows - group, group)], coef_low
     )
+    ocean_rows = rows // group
+    tiles = wet_list.shape[1]
+    owner = wet_owner[...]
+    mine = lax.broadcasted_iota(jnp.int32, (count, tiles), 0) == owner
+    before = lax.broadcasted_iota(jnp.int32, (tiles, tiles), 0) < lax.broadcasted_iota(
+        jnp.int32, (tiles, tiles), 1
+    )
+    mine = mine.astype(jnp.float32)
+    earlier = jnp.sum(mine * dot(mine, before.astype(jnp.float32)), axis=0, keepdims=True)
+    slot = lax.broadcasted_iota(jnp.int32, (slots, tiles), 0)
+    filled = (slot // PAD == owner) & ((slot % PAD).astype(jnp.float32) == earlier)
+    row = lax.broadcasted_iota(jnp.int32, (rows, tiles), 0)
+    placed = (row // group * width + row % group == wet_list[...]) & (row % group < width)
+    select[...] = lax.dot_general(
+        filled.astype(jnp.float32), placed.astype(jnp.float32), (((1,), (1,)), ((), ())),
+        precision=HIGHEST, preferred_element_type=jnp.float32,
+    )
+    lat = lax.broadcasted_iota(jnp.int32, mat.shape, 0)
+    row = lax.broadcasted_iota(jnp.int32, mat.shape, 1)
+    lat_of = jnp.where(lat % group == row % group, lat // group, -1) + (me * LAT_DEV - 1)
+    lat_of = jnp.where(lat % group == row % group, lat_of, -9)
+    row_of = row // group + me * ocean_rows
+    table = jnp.zeros(mat.shape, jnp.float32)
+    for e in range(remap_src.shape[0]):
+        hit = (lat_of == remap_tgt[e]) & (row_of == remap_src[e])
+        table = table + jnp.where(hit, remap_weight[e], 0.0)
+    mat[...] = table
     slot = lax.broadcasted_iota(jnp.int32, (slots, count * capacity), 0)
     cell = lax.broadcasted_iota(jnp.int32, (slots, count * capacity), 1)
     rank = slot % PAD
@@ -211,7 +241,7 @@
         air[hour] = dot(widen, air_in[hour, 0])
         wind[hour] = dot(widen, wind_in[hour, 0])
 
-    def advance(hour, old, new):
+    def advance(hour, old, new, first, end):
         def level(l, carry):
             xs = [old[l + 1, c] for c in range(4)]
             for c in range(4):
@@ -226,15 +256,32 @@
                 )
             return carry
 
-        lax.fori_loop(0, levels, level, 0)
+        lax.fori_loop(first, end, level, 0)
+
+    def turn(state, result, first, end):
+        def level(l, carry):
+            for c in range(4):
+                result[l + 1, c] = cost[...] * cost[...] * (state[l + 1, c] - target[l, c])
+            return carry
+
+        lax.fori_loop(first, end, level, 0)
 
     old, new = field_a, field_b
+    finish(waiting)
+    advance(0, old, new, 0, levels)
     for hour in range(hours):
-        finish(waiting)
-        advance(hour, old, new)
         more = hour + 1 < hours
-        waiting = halo(new, hour + 1, 1, levels - 1) if more else []
-        got = swap(dot(select[...], surface(new)))
+        rest = halo(new, hour + 1, 1, levels - 1) if more else []
+
+        def beside():
+            if more:
+                finish(rest)
+                advance(hour + 1, new, old, 2, levels)
+            else:
+                turn(new, old, 1, levels)
+                rest.extend(halo(old, hours, 1, levels - 1))
+
+        got = swap(dot(select[...], surface(new)), beside)
         mixed = jnp.tanh(dot(mix[...], got))
         mixed_s[hour] = mixed
         contrast = []
@@ -253,18 +300,15 @@
         atmos_s[hour] = total
         new[1, 0] = new[1, 0] + FEEDBACK * dot_t(mat[...], total)
         if more:
-            waiting += halo(new, hour + 1, 0, 1)
-        old, new = new, old
-
-    def turn(l, carry):
-        for c in range(4):
-            new[l + 1, c] = cost[...] * cost[...] * (old[l + 1, c] - target[l, c])
-        return carry
-
-    lax.fori_loop(0, levels, turn, 0)
-    old, new = new, old
-
-    def retreat(hour, at, old, new, last):
+            top = halo(new, hour + 1, 0, 1)
+            advance(hour + 1, new, old, 1, 2)
+            finish(top)
+            advance(hour + 1, new, old, 0, 1)
+            old, new = new, old
+        else:
+            turn(new, old, 0, 1)
+
+    def retreat(hour, at, old, new, first, end, carry):
         real = lax.rem(lax.broadcasted_iota(jnp.int32, (rows, 128), 0), group) < width
         factor = coef[...]
 
@@ -288,21 +332,27 @@
                     + TIME_STEP * sum(chan[l * 16 + c * 4 + k] * weighted[c] for c in range(4))
                 )
                 new[l + 1, k] = result
-                if last:
+                if hour == 0:
                     pg = pg + pert[l, k] * result
                     gg = gg + result * result
             return pg, gg
 
-        start = jnp.zeros((rows, 128), jnp.float32)
-        return lax.fori_loop(0, levels, level, (start, start))
+        return lax.fori_loop(first, end, level, carry)
+
+    none = jnp.zeros((rows, 128), jnp.float32)
+    sofar = [(none, none)]
 
     for hour in reversed(range(hours)):
         at = 2 * hours - 1 - hour
         total = FEEDBACK * remap(old)
-        waiting = halo(old, at, 1, levels - 1)
         total = total * (1.0 - atmos_s[hour] * atmos_s[hour])
         old[1, 0] = old[1, 0] + dot_t(mat[...], total)
-        got = swap(dot(select[...], surface(old)))
+
+        def beside_adjoint():
+            finish(rest)
+            sofar[0] = retreat(hour, at, old, new, 2, levels, sofar[0])
+
+        got = swap(dot(select[...], surface(old)), beside_adjoint)
         scaled = FLUX_RATE * wind[hour]
         dforce = []
         for c in range(4):
@@ -314,10 +364,14 @@
         held = mixed_s[hour]
         back = swap(signed + dot_t(mix[...], (1.0 - held * held) * joined))
         add_surface(old, dot_t(select[...], back))
-        waiting += halo(old, at, 0, 1)
-        finish(waiting)
-        pg, gg = retreat(hour, at, old, new, hour == 0)
+        top = halo(old, at, 0, 1)
+        sofar[0] = retreat(hour, at, old, new, 1, 2, sofar[0])
+        if hour > 0:
+            rest = halo(new, at + 1, 1, levels - 1)
+        finish(top)
+        sofar[0] = retreat(hour, at, old, new, 0, 1, sofar[0])
         old, new = new, old
+    pg, gg = sofar[0]
 
     for i, value in enumerate((pp, pg, gg)):
         value = value if value.ndim == 2 else jnp.sum(value, axis=0)
@@ -383,9 +437,7 @@
     remap_weight,
 ):
     count = lax.axis_size("horiz")
-    me = lax.axis_index("horiz")
     levels, row_count, _, cells = base_state.shape
-    tile_total = wet_list.shape[1]
     hour_count = air_temp.shape[0]
     width = cells // 128
     group = -(-width // 8) * 8
@@ -393,29 +445,6 @@
     slots = count * PAD
     lat_rows = (LAT_DEV + 2) * group
 
-    owner = wet_owner[0]
-    entry = jnp.arange(tile_total, dtype=jnp.int32)
-    same = (owner[:, None] == owner[None, :]) & (entry[None, :] < entry[:, None])
-    rank = jnp.sum(same.astype(jnp.int32), axis=1)
-    slot = jnp.where(owner >= 0, owner * PAD + rank, -1)
-    to_slot = (slot[None, :] == jnp.arange(slots, dtype=jnp.int32)[:, None]).astype(jnp.float32)
-    place = jnp.where(owner >= 0, wet_list[0] // width * group + wet_list[0] % width, -1)
-    of_tile = (place[:, None] == jnp.arange(rows, dtype=jnp.int32)[None, :]).astype(jnp.float32)
-    select = dot(to_slot, of_tile)
-
-    src = remap_src - me * row_count
-    tgt = remap_tgt - (me * LAT_DEV - 1)
-    hit_src = (src[:, None] == jnp.arange(row_count, dtype=jnp.int32)[None, :]).astype(jnp.float32)
-    hit_tgt = (tgt[:, None] == jnp.arange(LAT_DEV + 2, dtype=jnp.int32)[None, :]).astype(
-        jnp.float32
-    )
-    small = jnp.sum(
-        hit_tgt[:, :, None] * hit_src[:, None, :] * remap_weight[:, None, None], axis=0
-    )
-    index = jnp.arange(group, dtype=jnp.int32)
-    eye = (index[:, None] == index[None, :]).astype(jnp.float32)
-    mat = (small[:, None, :, None] * eye[None, :, None, :]).reshape(lat_rows, rows)
-
     def to_tiles(field):
         pieces = field.reshape(levels, row_count, 4, width, 128).transpose(0, 2, 1, 3, 4)
         widths = ((0, 0), (0, 0), (0, 0), (0, group - width), (0, 0))
@@ -429,11 +458,11 @@
     rounds = 2 * hour_count
     operands = (
         to_tiles(perturbation), to_tiles(base_state), to_tiles(target_state),
-        column_tiles(cost_weight), column_tiles(diffusivity), select, mat, owner_mix, air_temp,
-        wind_speed, chan_mix.reshape(-1), coupler_mix,
-    )
-    specs = [pl.BlockSpec(memory_space=pltpu.VMEM)] * (len(operands) - 2)
-    specs += [pl.BlockSpec(memory_space=pltpu.SMEM)] * 2
+        column_tiles(cost_weight), column_tiles(diffusivity), wet_list, wet_owner, owner_mix, air_temp,
+        wind_speed, chan_mix.reshape(-1), coupler_mix, remap_src, remap_tgt, remap_weight,
+    )
+    specs = [pl.BlockSpec(memory_space=pltpu.VMEM)] * (len(operands) - 5)
+    specs += [pl.BlockSpec(memory_space=pltpu.SMEM)] * 5
     result = pl.pallas_call(
         functools.partial(
             whole_kernel, count, width, group, hour_count, perturbation.size * count
@@ -442,6 +471,8 @@
         in_specs=specs,
         out_specs=pl.BlockSpec(memory_space=pltpu.VMEM),
         scratch_shapes=[
+            pltpu.VMEM((slots, rows), f32),
+            pltpu.VMEM((lat_rows, rows), f32),
             pltpu.VMEM((slots, slots), f32),
             pltpu.VMEM((hour_count, slots, 128), f32),
             pltpu.VMEM((hour_count, slots, 128), f32),

time: 128 us -> 116 us (0.906)
  Pallas kernels: 109 us -> 101 us
  other arithmetic: 4.42 us -> 0 us
    pallas_call x1, Pallas kernels: 109 us -> 101 us  [body(): pl.pallas_call(functools.partial(whole_kernel, count, width, group, hour_...]
    reduce_sum x2 -> x0, other arithmetic: 1.65 us -> none  [the longest x1 0.91 us: body(): rank = jnp.sum(same.astype(jnp.int32), axis=1)]
    sub x2 -> x0, other arithmetic: 1.31 us -> none  [the longest x1 0.66 us: body(): tgt = remap_tgt - (me * LAT_DEV - 1)]
    unnamed x12 -> x22, local copies, waits for them, and re-layouts: 3.18 us -> 3.22 us
where the time goes in v4:
time: 116 us; the launch traced here: 115 us
  Pallas kernels  101 us (87%)
  local copies, waits for them, and re-layouts  13.7 us (12%)
    pallas_call x1, Pallas kernels, body(): pl.pallas_call(functools.partial(whole_kernel, count, width, group, hour_...  101 us
    reshape x3, local copies, waits for them, and re-layouts, to_tiles(): field.reshape(levels, row_count, 4, width, 128).transpose(0, 2, 1, 3, 4)  6.63 us
    unnamed x22, local copies, waits for them, and re-layouts  3.22 us

profile of v4, /device:TPU:0, one launch (start us, length us, event | category | flops | bytes accessed | tf_op | source)
XLA Modules:
  0.0 115.1 jit_solution(11701946448859378307)
XLA Ops:
  0.0 0.8 copy.27
  0.8 0.1 reshape.49.chan
  0.9 0.8 reshape.45
  1.8 0.8 reshape.47
  2.6 1.9 %reshape.52 = f32[8,5,4,15,128]{4,3,2,1,0:T(8,128)S(1)} reshape(f32[8,5,4,1920]{3,2,1,0:T(4,128)} %param.15) | data formatting | bytes 2457600 | tf_op jit(solution)/shard_map/reshape | solution.py:449
  4.5 0.1 copy.34
  4.7 0.1 pad.17.clone
  4.8 1.9 %reshape.53 = f32[8,5,4,15,128]{4,3,2,1,0:T(8,128)S(1)} reshape(f32[8,5,4,1920]{3,2,1,0:T(4,128)} %param.16) | data formatting | bytes 2457600 | tf_op jit(solution)/shard_map/reshape | solution.py:449
  6.7 0.1 copy.35
  6.9 0.1 pad.18.clone
  7.0 2.8 %reshape.54 = f32[8,5,4,15,128]{4,3,2,1,0:T(8,128)} reshape(f32[8,5,4,1920]{3,2,1,0:T(4,128)} %param.17) | data formatting | bytes 2457600 | tf_op jit(solution)/shard_map/reshape | solution.py:449
  9.8 1.4 %copy.36 = f32[8,4,5,15,128]{4,3,2,1,0:T(8,128)S(1)} copy(f32[8,4,5,15,128]{4,3,1,2,0:T(8,128)} %bitcast.24) | data formatting | bytes 2457600
  11.2 0.0 copy-start
  11.3 0.0 copy-start.1
  11.3 0.0 copy-start.2
  11.3 0.0 copy-start.3
  11.3 0.0 copy-start.4
  11.3 0.0 copy-start.5
  11.3 0.0 copy-start.6
  11.3 0.0 copy-start.7
  11.3 0.0 copy-start.8
  11.4 0.1 pad.19.clone
  11.5 0.7 copy-done
  12.1 0.0 copy-done.1
  12.2 0.0 copy-done.2
  12.2 0.0 copy-done.3
  12.2 0.0 copy-done.4
  12.2 0.0 copy-done.5
  12.2 0.0 copy-done.6
  12.2 0.0 copy-done.7
  12.2 0.0 copy-done.8
  12.2 101.2 %shard_map.145 = f32[8,4,80,128]{3,2,1,0:T(8,128)S(1)} custom-call(f32[8,4,80,128]{3,2,1,0:T(8,128)S(1)} %bitcast.17, f32[8,4,80,128]{3,2,1,0:T(8,128)S(1)} %bitcast.18, f32[8,4,80,128]{3,2,1,0:T(8,128)S(1)} %bitcast.19, f32[80,128]{1,0:T(8,128)S(1)} %bitcast.20, f32[80,128]{1,0:T(8,128)S(1)} %bitcast.21, s32[1,75]{1,0:T(1,128)S(1)} %copy-done.4, ...), custom_call_target="tpu_custom_call" | custom-call | tf_op jit(solution)/shard_map/pallas_call | solution.py:466
  113.4 0.1 copy_bitcast_fusion
  113.6 0.2 reshape.51
  113.8 1.3 %copy.29 = f32[8,5,4,1920]{3,2,1,0:T(4,128)} copy(f32[8,5,4,1920]{3,0,2,1:T(8,128)S(1)} %reshape.51) | data formatting | bytes 2457600 | tf_op jit(solution)/shard_map/reshape | solution.py:507
  (2 shorter events, 0.0 us)
Async XLA Ops:
  11.2 0.9 copy-start
  11.3 0.9 copy-start.1
  11.3 0.9 copy-start.2
  11.3 0.9 copy-start.3
  11.3 0.9 copy-start.4
  11.3 0.9 copy-start.5
  11.3 0.9 copy-start.6
  11.3 0.9 copy-start.7
  11.3 0.9 copy-start.8

commit v5 on v4

--- a/solution.py
+++ b/solution.py
@@ -271,17 +271,21 @@
     advance(0, old, new, 0, levels)
     for hour in range(hours):
         more = hour + 1 < hours
-        rest = halo(new, hour + 1, 1, levels - 1) if more else []
-
-        def beside():
+        rest = []
+
+        def beside_first():
+            if more:
+                rest.extend(halo(new, hour + 1, 1, levels - 1))
+            else:
+                turn(new, old, 1, levels)
+                rest.extend(halo(old, hours, 1, levels - 1))
+
+        def beside_second():
             if more:
                 finish(rest)
                 advance(hour + 1, new, old, 2, levels)
-            else:
-                turn(new, old, 1, levels)
-                rest.extend(halo(old, hours, 1, levels - 1))
-
-        got = swap(dot(select[...], surface(new)), beside)
+
+        got = swap(dot(select[...], surface(new)), beside_first)
         mixed = jnp.tanh(dot(mix[...], got))
         mixed_s[hour] = mixed
         contrast = []
@@ -294,7 +298,7 @@
         ]
         force_s[hour] = jnp.concatenate(force, axis=1)
         scaled = FLUX_RATE * wind[hour]
-        back = swap(jnp.concatenate([scaled * f for f in force], axis=1))
+        back = swap(jnp.concatenate([scaled * f for f in force], axis=1), beside_second)
         add_surface(new, dot_t(select[...], back))
         total = jnp.tanh(remap(new))
         atmos_s[hour] = total
@@ -348,11 +352,15 @@
         total = total * (1.0 - atmos_s[hour] * atmos_s[hour])
         old[1, 0] = old[1, 0] + dot_t(mat[...], total)
 
+        def start_rest():
+            if hour + 1 < hours:
+                rest.extend(halo(old, at, 1, levels - 1))
+
         def beside_adjoint():
             finish(rest)
             sofar[0] = retreat(hour, at, old, new, 2, levels, sofar[0])
 
-        got = swap(dot(select[...], surface(old)), beside_adjoint)
+        got = swap(dot(select[...], surface(old)), start_rest)
         scaled = FLUX_RATE * wind[hour]
         dforce = []
         for c in range(4):
@@ -362,12 +370,11 @@
         joined = jnp.concatenate(dcontrast, axis=1)
         signed = jnp.concatenate([-dcontrast[0]] + dcontrast[1:], axis=1)
         held = mixed_s[hour]
-        back = swap(signed + dot_t(mix[...], (1.0 - held * held) * joined))
+        back = swap(signed + dot_t(mix[...], (1.0 - held * held) * joined), beside_adjoint)
         add_surface(old, dot_t(select[...], back))
         top = halo(old, at, 0, 1)
         sofar[0] = retreat(hour, at, old, new, 1, 2, sofar[0])
-        if hour > 0:
-            rest = halo(new, at + 1, 1, levels - 1)
+        rest = []
         finish(top)
         sofar[0] = retreat(hour, at, old, new, 0, 1, sofar[0])
         old, new = new, old

time: 116 us -> 114 us (0.983)
  Pallas kernels: 101 us -> 99.4 us
    pallas_call x1, Pallas kernels: 101 us -> 99.4 us  [body(): pl.pallas_call(functools.partial(whole_kernel, count, width, group, hour_...]
where the time goes in v5:
time: 114 us; the launch traced here: 113 us
  Pallas kernels  99.4 us (87%)
  local copies, waits for them, and re-layouts  13.7 us (12%)
    pallas_call x1, Pallas kernels, body(): pl.pallas_call(functools.partial(whole_kernel, count, width, group, hour_...  99.4 us
    reshape x3, local copies, waits for them, and re-layouts, to_tiles(): field.reshape(levels, row_count, 4, width, 128).transpose(0, 2, 1, 3, 4)  6.63 us
    unnamed x22, local copies, waits for them, and re-layouts  3.22 us

profile of v5, /device:TPU:0, one launch (start us, length us, event | category | flops | bytes accessed | tf_op | source)
XLA Modules:
  0.0 113.4 jit_solution(1039658321737299911)
XLA Ops:
  0.0 0.8 copy.27
  0.8 0.1 reshape.49.chan
  0.9 0.8 reshape.45
  1.8 0.8 reshape.47
  2.6 1.9 %reshape.52 = f32[8,5,4,15,128]{4,3,2,1,0:T(8,128)S(1)} reshape(f32[8,5,4,1920]{3,2,1,0:T(4,128)} %param.15) | data formatting | bytes 2457600 | tf_op jit(solution)/shard_map/reshape | solution.py:456
  4.5 0.1 copy.34
  4.7 0.1 pad.17.clone
  4.8 1.9 %reshape.53 = f32[8,5,4,15,128]{4,3,2,1,0:T(8,128)S(1)} reshape(f32[8,5,4,1920]{3,2,1,0:T(4,128)} %param.16) | data formatting | bytes 2457600 | tf_op jit(solution)/shard_map/reshape | solution.py:456
  6.7 0.1 copy.35
  6.9 0.1 pad.18.clone
  7.0 2.8 %reshape.54 = f32[8,5,4,15,128]{4,3,2,1,0:T(8,128)} reshape(f32[8,5,4,1920]{3,2,1,0:T(4,128)} %param.17) | data formatting | bytes 2457600 | tf_op jit(solution)/shard_map/reshape | solution.py:456
  9.8 1.4 %copy.36 = f32[8,4,5,15,128]{4,3,2,1,0:T(8,128)S(1)} copy(f32[8,4,5,15,128]{4,3,1,2,0:T(8,128)} %bitcast.24) | data formatting | bytes 2457600
  11.2 0.0 copy-start
  11.3 0.0 copy-start.1
  11.3 0.0 copy-start.2
  11.3 0.0 copy-start.3
  11.3 0.0 copy-start.4
  11.3 0.0 copy-start.5
  11.3 0.0 copy-start.6
  11.3 0.0 copy-start.7
  11.3 0.0 copy-start.8
  11.4 0.1 pad.19.clone
  11.5 0.7 copy-done
  12.1 0.0 copy-done.1
  12.2 0.0 copy-done.2
  12.2 0.0 copy-done.3
  12.2 0.0 copy-done.4
  12.2 0.0 copy-done.5
  12.2 0.0 copy-done.6
  12.2 0.0 copy-done.7
  12.2 0.0 copy-done.8
  12.2 99.4 %shard_map.145 = f32[8,4,80,128]{3,2,1,0:T(8,128)S(1)} custom-call(f32[8,4,80,128]{3,2,1,0:T(8,128)S(1)} %bitcast.17, f32[8,4,80,128]{3,2,1,0:T(8,128)S(1)} %bitcast.18, f32[8,4,80,128]{3,2,1,0:T(8,128)S(1)} %bitcast.19, f32[80,128]{1,0:T(8,128)S(1)} %bitcast.20, f32[80,128]{1,0:T(8,128)S(1)} %bitcast.21, s32[1,75]{1,0:T(1,128)S(1)} %copy-done.4, ...), custom_call_target="tpu_custom_call" | custom-call | tf_op jit(solution)/shard_map/pallas_call | solution.py:473
  111.7 0.1 copy_bitcast_fusion
  111.8 0.2 reshape.51
  112.0 1.3 %copy.29 = f32[8,5,4,1920]{3,2,1,0:T(4,128)} copy(f32[8,5,4,1920]{3,0,2,1:T(8,128)S(1)} %reshape.51) | data formatting | bytes 2457600 | tf_op jit(solution)/shard_map/reshape | solution.py:514
  (2 shorter events, 0.0 us)
Async XLA Ops:
  11.2 0.9 copy-start
  11.3 0.9 copy-start.1
  11.3 0.9 copy-start.2
  11.3 0.9 copy-start.3
  11.3 0.9 copy-start.4
  11.3 0.9 copy-start.5
  11.3 0.9 copy-start.6
  11.3 0.9 copy-start.7
  11.3 0.9 copy-start.8
